TPU v7x, 32 devices: a whole 2x2x4 slice. The times are simulated.
32 devices in a mesh: dp: 4 (over y, x), blk: 8 (over z, core).
Axes of the slice: x: 2, y: 2, z: 4, core: 2. Of those that a mesh axis runs over, the one named last changes fastest.
Arguments:
- tokens: bfloat16 [1280, 3072], P(('dp', 'blk')), may hold values from -6 to 6
- expert_ids: int32 [1280, 2], P(('dp', 'blk')), may hold values from 0 to 7, as said below
- route_probs: float32 [1280, 2], P(('dp', 'blk')), may hold values from 0.2 to 1
- scale_exps: int32 [3], replicated, may hold values from -2 to 2
- w_gate: bfloat16 [3072, 8192], P(None, 'blk'), may hold values from -0.109375 to 0.109375
- w_up: bfloat16 [3072, 8192], P(None, 'blk'), may hold values from -0.109375 to 0.109375
- w_down: bfloat16 [8192, 3072], P('blk'), may hold values from -0.0625 to 0.0625
- out_grad: bfloat16 [1280, 3072], P(('dp', 'blk')), may hold values from -6 to 6
Outputs:
- mixed: bfloat16 [1280, 3072], P(('dp', 'blk'))
- input_grad: bfloat16 [1280, 3072], P(('dp', 'blk'))
- grad_gate: bfloat16 [3072, 8192], P('dp', 'blk')
- grad_up: bfloat16 [3072, 8192], P('dp', 'blk')
- grad_down: bfloat16 [8192, 3072], P('blk', 'dp')
Inputs may be any that keep to these rules, and one draw needn't show every extreme that they name: `expert_ids`: the tokens are those dispatched to expert 0: each row names expert 0 and one other expert; the layer computes expert 0.
All inputs are finite; a program needn't handle non-finite values.
Results may differ from a plain program's by a relative error of at most 0.019.
Values may be sent and summed in bfloat16 or wider, within the bound.
A program may use at most 128 MiB of HBM per device.

v0:
```python
import jax
import jax.numpy as jnp
from jax import lax
from jax.sharding import PartitionSpec as P


def contract_rows(left, right):
    return lax.dot_general(
        left, right, (((0,), (0,)), ((), ())), preferred_element_type=jnp.float32
    )


def contract_cols(left, right):
    return lax.dot_general(
        left, right, (((1,), (1,)), ((), ())), preferred_element_type=jnp.float32
    )


def local(tokens, expert_ids, route_probs, scale_exps, w_gate, w_up, w_down, out_grad):
    scales = jnp.exp2(scale_exps.astype(jnp.float32))
    combine = jnp.sum(jnp.where(expert_ids == 0, route_probs, jnp.zeros_like(route_probs)), axis=1)[
        :, None
    ]
    gathered = lax.all_gather(tokens, "blk", axis=0, tiled=True)
    gate_pre = jnp.dot(gathered, w_gate, preferred_element_type=jnp.float32) * scales[0]
    up_pre = jnp.dot(gathered, w_up, preferred_element_type=jnp.float32) * scales[1]
    sigmoid_gate = jax.nn.sigmoid(gate_pre)
    hidden = (gate_pre * sigmoid_gate * up_pre).astype(jnp.bfloat16)
    expert_out = lax.psum_scatter(
        (jnp.dot(hidden, w_down, preferred_element_type=jnp.float32) * scales[2]).astype(
            jnp.bfloat16
        ),
        "blk",
        scatter_dimension=0,
        tiled=True,
    ).astype(jnp.float32)
    mixed = (combine * expert_out).astype(jnp.bfloat16)
    scaled = (combine * out_grad.astype(jnp.float32)).astype(jnp.bfloat16)
    scaled_all = lax.all_gather(scaled, "blk", axis=0, tiled=True)
    d_hidden = contract_cols(scaled_all, w_down) * scales[2]
    d_gate = (d_hidden * up_pre * sigmoid_gate * (1.0 + gate_pre * (1.0 - sigmoid_gate))).astype(
        jnp.bfloat16
    )
    d_up = (d_hidden * gate_pre * sigmoid_gate).astype(jnp.bfloat16)
    input_grad = lax.psum_scatter(
        (contract_cols(d_gate, w_gate) * scales[0] + contract_cols(d_up, w_up) * scales[1]).astype(
            jnp.bfloat16
        ),
        "blk",
        scatter_dimension=0,
        tiled=True,
    )
    term_gate = contract_rows(gathered, d_gate) * scales[0]
    term_up = contract_rows(gathered, d_up) * scales[1]
    term_down = contract_rows(hidden, scaled_all) * scales[2]
    grad_gate, grad_up, grad_down = (
        lax.psum_scatter(
            term_gate.astype(jnp.bfloat16), "dp", scatter_dimension=0, tiled=True
        ).astype(jnp.float32),
        lax.psum_scatter(
            term_up.astype(jnp.bfloat16), "dp", scatter_dimension=0, tiled=True
        ).astype(jnp.float32),
        lax.psum_scatter(
            term_down.astype(jnp.bfloat16), "dp", scatter_dimension=1, tiled=True
        ).astype(jnp.float32),
    )
    return (
        mixed,
        input_grad,
        grad_gate.astype(jnp.bfloat16),
        grad_up.astype(jnp.bfloat16),
        grad_down.astype(jnp.bfloat16),
    )


def solution(mesh):
    return jax.shard_map(
        local,
        mesh=mesh,
        in_specs=(
            P(("dp", "blk"), None),
            P(("dp", "blk"), None),
            P(("dp", "blk"), None),
            P(),
            P(None, "blk"),
            P(None, "blk"),
            P("blk", None),
            P(("dp", "blk"), None),
        ),
        out_specs=(
            P(("dp", "blk"), None),
            P(("dp", "blk"), None),
            P("dp", "blk"),
            P("dp", "blk"),
            P("blk", "dp"),
        ),
        check_vma=False,
    )
```

profile of v0, /device:TPU:0, one launch (start us, length us, event | category | flops | bytes accessed | tf_op | source)
XLA Modules:
  0.0 383.4 jit_solution(153031210221080803)
XLA Ops:
  7.2 0.7 fusion.5
  7.9 1.7 multiply_convert_fusion.6
  9.7 0.0 all-gather.3.cloned.1.call-start
  9.7 0.7 all-gather.3.cloned.1.call-update
  10.4 0.0 reduce-scatter.6.cloned.1.call-start
  10.5 0.7 multiply_exponential_fusion
  11.2 0.6 fusion.6
  11.8 29.2 %all-gather.5.cloned.1.call-done = bf16[320,3072]{1,0:T(8,128)(2,1)} async-done(((bf16[40,3072]{1,0:T(8,128)(2,1)}), bf16[320,3072]{1,0:T(8,128)(2,1)}) %all-gather.5.cloned.1.call-update) | async-done | bytes 1966096 | tf_op jit(solution)/shard_map/all_gather | solution.py:39
  41.0 7.5 %convolution_multiply_fusion.3 = f32[320,1024]{1,0:T(8,128)} fusion(bf16[320,3072]{1,0:T(8,128)(2,1)} %all-gather.5.cloned.1.call-done, bf16[1024,3072]{1,0:T(8,128)(2,1)} %param.14, f32[]{:T(128)} %bitcast.2), kind=kOutput, calls=%fused_computation.11 | convolution fusion | flops 2013593600 | bytes 9568260 | tf_op jit(solution)/shard_map/dot_general | solution.py:14
  48.4 21.7 %all-gather.3.cloned.1.call-done = bf16[320,3072]{1,0:T(8,128)(2,1)} async-done(((bf16[40,3072]{1,0:T(8,128)(2,1)}), bf16[320,3072]{1,0:T(8,128)(2,1)}) %all-gather.3.cloned.1.call-update) | async-done | bytes 1966096 | tf_op jit(solution)/shard_map/all_gather | solution.py:24
  70.2 6.8 %convolution_multiply_fusion.4 = f32[320,1024]{1,0:T(8,128)S(1)} fusion(bf16[320,3072]{1,0:T(8,128)(2,1)} %all-gather.3.cloned.1.call-done, bf16[3072,1024]{1,0:T(8,128)(2,1)} %param.13, f32[]{:T(128)} %bitcast.1), kind=kOutput, calls=%fused_computation.12 | convolution fusion | flops 2013593600 | bytes 9568260 | tf_op jit(solution)/shard_map/dot_general | solution.py:26
  77.0 4.5 %multiply_convert_fusion.4 = (bf16[320,1024]{1,0:T(8,128)(2,1)S(1)}, bf16[320,1024]{1,0:T(8,128)(2,1)S(1)}, bf16[320,1024]{1,0:T(8,128)(2,1)}) fusion(f32[320,1024]{1,0:T(8,128)S(1)} %copy-done.4, f32[320,1024]{1,0:T(8,128)S(1)} %convolution_multiply_fusion.4, f32[]{:T(128)} %bitcast, bf16[320,3072]{1,0:T(8,128)(2,1)S(1)} %copy-done.1, ...), kind=kOutput, calls=%fused_computation.15 | convolution fusion | flops 2018836480 | bytes 12845060 | tf_op jit(solution)/shard_map/dot_general | solution.py:25
  81.5 4.2 %fusion.4 = bf16[320,3072]{1,0:T(8,128)(2,1)} fusion(bf16[320,1024]{1,0:T(8,128)(2,1)S(1)} %get-tuple-element.11, bf16[1024,3072]{1,0:T(8,128)(2,1)S(1)} %bitcast.26, f32[]{:T(128)} %bitcast.2), kind=kOutput, calls=%fused_computation.10 | convolution fusion | flops 2015232000 | bytes 8912900 | tf_op jit(solution)/shard_map/dot_general | solution.py:30
  85.7 0.0 reduce-scatter.10.cloned.1.call-start
  85.8 1.5 copy-done.2
  87.2 6.2 %fusion = bf16[3072,1024]{0,1:T(8,128)(2,1)} fusion(f32[]{:T(128)} %bitcast, bf16[320,1024]{1,0:T(8,128)(2,1)S(1)} %get-tuple-element.10, bf16[320,3072]{1,0:T(8,128)(2,1)S(1)} %copy-done.2), kind=kOutput, calls=%fused_computation.3 | convolution fusion | flops 2019557376 | bytes 8912900 | tf_op jit(solution)/shard_map/dot_general | solution.py:8
  93.5 0.0 reduce-scatter.12.cloned.1.call-start
  93.5 7.1 %fusion.1 = bf16[3072,1024]{0,1:T(8,128)(2,1)} fusion(f32[]{:T(128)} %bitcast.1, bf16[320,1024]{1,0:T(8,128)(2,1)} %get-tuple-element.12, bf16[320,3072]{1,0:T(8,128)(2,1)S(1)} %copy-done.2), kind=kOutput, calls=%fused_computation.4 | convolution fusion | flops 2019557376 | bytes 8912900 | tf_op jit(solution)/shard_map/dot_general | solution.py:8
  100.7 0.2 reduce-scatter.8.cloned.1.call-start
  100.9 0.8 copy-done.3
  101.7 5.7 %convolution_multiply_fusion = f32[320,3072]{1,0:T(8,128)S(1)} fusion(bf16[320,1024]{1,0:T(8,128)(2,1)S(1)} %copy-done.3, bf16[3072,1024]{1,0:T(8,128)(2,1)} %param.13, f32[]{:T(128)} %bitcast.1), kind=kOutput, calls=%fused_computation.5 | convolution fusion | flops 2014248960 | bytes 10878980 | tf_op jit(solution)/shard_map/dot_general | solution.py:14
  107.4 7.0 %fusion.3 = bf16[320,3072]{1,0:T(8,128)(2,1)} fusion(f32[320,3072]{1,0:T(8,128)S(1)} %convolution_multiply_fusion, bf16[320,1024]{1,0:T(8,128)(2,1)S(1)} %get-tuple-element.10, bf16[3072,1024]{1,0:T(8,128)(2,1)} %param.12, f32[]{:T(128)} %bitcast), kind=kOutput, calls=%fused_computation.9 | convolution fusion | flops 2016215040 | bytes 12845060 | tf_op jit(solution)/shard_map/dot_general | solution.py:14
  114.5 0.0 reduce-scatter.14.cloned.1.call-start
  114.5 1.5 copy-done
  116.0 6.3 %multiply_convert_fusion = bf16[1024,3072]{1,0:T(8,128)(2,1)} fusion(bf16[320,1024]{1,0:T(8,128)(2,1)S(1)} %get-tuple-element.11, bf16[320,3072]{1,0:T(8,128)(2,1)S(1)} %copy-done, f32[]{:T(128)} %bitcast.2), kind=kOutput, calls=%fused_computation | convolution fusion | flops 2019557376 | bytes 8912900 | tf_op jit(solution)/shard_map/dot_general | solution.py:8
  122.4 1.7 multiply_convert_fusion.7
  124.1 68.4 %reduce-scatter.10.cloned.1.call-done = bf16[768,1024]{0,1:T(8,128)(2,1)} async-done(((bf16[3072,1024]{0,1:T(8,128)(2,1)}), bf16[768,1024]{0,1:T(8,128)(2,1)}) %reduce-scatter.10.cloned.1.call-update) | async-done | bytes 1572880 | tf_op jit(solution)/shard_map/reduce_scatter | solution.py:57
  192.5 2.6 copy.13
  195.1 70.8 %reduce-scatter.12.cloned.1.call-done = bf16[768,1024]{0,1:T(8,128)(2,1)} async-done(((bf16[3072,1024]{0,1:T(8,128)(2,1)}), bf16[768,1024]{0,1:T(8,128)(2,1)}) %reduce-scatter.12.cloned.1.call-update) | async-done | bytes 1572880 | tf_op jit(solution)/shard_map/reduce_scatter | solution.py:60
  265.9 2.6 copy.14
  268.4 35.8 %reduce-scatter.8.cloned.1.call-done = bf16[40,3072]{1,0:T(8,128)(2,1)} async-done(((bf16[320,3072]{1,0:T(8,128)(2,1)}), bf16[40,3072]{1,0:T(8,128)(2,1)}) %reduce-scatter.8.cloned.1.call-update) | async-done | bytes 245776 | tf_op jit(solution)/shard_map/reduce_scatter | solution.py:45
  304.2 72.3 %reduce-scatter.14.cloned.1.call-done = bf16[1024,768]{1,0:T(8,128)(2,1)} async-done(((bf16[1024,3072]{1,0:T(8,128)(2,1)}), bf16[1024,768]{1,0:T(8,128)(2,1)}) %reduce-scatter.14.cloned.1.call-update) | async-done | bytes 1572880 | tf_op jit(solution)/shard_map/reduce_scatter | solution.py:63
  (25 shorter events, 0.2 us)
Async XLA Ops:
  7.2 33.8 %all-gather.5.cloned.1.call-start = ((), (), s32[]{:S(2)}) async-start(), calls=%async_computation.7 | async-start | bytes 2211840 | tf_op jit(solution)/shard_map/all_gather | solution.py:39
  9.7 60.5 %all-gather.3.cloned.1.call-start = ((), (), s32[]{:S(2)}) async-start(), calls=%async_computation.5 | async-start | bytes 2211840 | tf_op jit(solution)/shard_map/all_gather | solution.py:24
  10.4 111.9 %reduce-scatter.6.cloned.1.call-start = ((), (), s32[]{:S(2)}) async-start(), calls=%async_computation.6 | async-start | bytes 2211840 | tf_op jit(solution)/shard_map/reduce_scatter | solution.py:29
  41.0 36.0 %slice-start.2 = ((s8[6291456]{0:T(1024)(128)(4,1)}), s8[2097152]{0:T(1024)(128)(4,1)S(1)}, s32[]{:S(2)}) async-start(s8[6291456]{0:T(1024)(128)(4,1)} %bitcast.27), calls=%async_computation.14 | async-start | bytes 4194304
  70.2 6.8 %slice-start.3 = ((s8[6291456]{0:T(1024)(128)(4,1)}), s8[4194304]{0:T(1024)(128)(4,1)S(1)}, s32[]{:S(2)}) async-start(s8[6291456]{0:T(1024)(128)(4,1)} %bitcast.27), calls=%async_computation.15 | async-start | bytes 8388608
  70.2 6.8 %copy-start.1 = (bf16[320,3072]{1,0:T(8,128)(2,1)S(1)}, bf16[320,3072]{1,0:T(8,128)(2,1)}, u32[]{:S(2)}) copy-start(bf16[320,3072]{1,0:T(8,128)(2,1)} %all-gather.3.cloned.1.call-done) | copy-start | bytes 5898244
  70.2 6.8 %copy-start.4 = (f32[320,1024]{1,0:T(8,128)S(1)}, f32[320,1024]{1,0:T(8,128)}, u32[]{:S(2)}) copy-start(f32[320,1024]{1,0:T(8,128)} %convolution_multiply_fusion.3) | copy-start | bytes 3932164
  70.2 11.3 %slice-start = ((s8[6291456]{0:T(1024)(128)(4,1)}), s8[4194304]{0:T(1024)(128)(4,1)S(1)}, s32[]{:S(2)}) async-start(s8[6291456]{0:T(1024)(128)(4,1)} %bitcast.25), calls=%async_computation.12 | async-start | bytes 8388608
  77.0 4.5 %slice-start.1 = ((s8[6291456]{0:T(1024)(128)(4,1)}), s8[2097152]{0:T(1024)(128)(4,1)S(1)}, s32[]{:S(2)}) async-start(s8[6291456]{0:T(1024)(128)(4,1)} %bitcast.25), calls=%async_computation.13 | async-start | bytes 4194304
  85.7 1.5 copy-start.2
  85.7 106.8 %reduce-scatter.10.cloned.1.call-start = ((), (), s32[]{:S(2)}) async-start(), calls=%async_computation.9 | async-start | bytes 7864320 | tf_op jit(solution)/shard_map/reduce_scatter | solution.py:57
  93.5 172.4 %reduce-scatter.12.cloned.1.call-start = ((), (), s32[]{:S(2)}) async-start(), calls=%async_computation.10 | async-start | bytes 7864320 | tf_op jit(solution)/shard_map/reduce_scatter | solution.py:60
  100.6 1.1 copy-start.3
  100.7 203.6 %reduce-scatter.8.cloned.1.call-start = ((), (), s32[]{:S(2)}) async-start(), calls=%async_computation.8 | async-start | bytes 2211840 | tf_op jit(solution)/shard_map/reduce_scatter | solution.py:45
  114.5 1.6 copy-start
  114.5 262.0 %reduce-scatter.14.cloned.1.call-start = ((), (), s32[]{:S(2)}) async-start(), calls=%async_computation.11 | async-start | bytes 7864320 | tf_op jit(solution)/shard_map/reduce_scatter | solution.py:63
Sparse Core Ops, SparseCore 0:
  10.2 30.7 all-gather.4
  42.6 27.5 all-gather.2
  85.8 35.0 reduce-scatter.5
  124.1 68.4 reduce-scatter.9
  195.6 70.1 reduce-scatter.11
  268.7 35.4 reduce-scatter.7
  307.8 68.6 reduce-scatter.13
where the time goes:
time: 384 us; the launch traced here: 383 us
  waiting for transfers between devices  299 us (78%)
  matrix products  55.2 us (14%)
  between operations  14.2 us (4%)
  local copies, waits for them, and re-layouts  9.58 us (2%)
  other arithmetic  4.87 us (1%)
    reduce_scatter x1, waiting for transfers between devices, local(): lax.psum_scatter(term_down.astype(jnp.bfloat16), 'dp', scatter_dimension=...  72.3 us
    reduce_scatter x1, waiting for transfers between devices, local(): lax.psum_scatter(term_up.astype(jnp.bfloat16), 'dp', scatter_dimension=0,...  70.8 us
    reduce_scatter x1, waiting for transfers between devices, local(): lax.psum_scatter(term_gate.astype(jnp.bfloat16), 'dp', scatter_dimension=...  68.4 us
    reduce_scatter x1, waiting for transfers between devices, local(): lax.psum_scatter((contract_cols(d_gate, w_gate) * scales[0] + contract_co...  35.8 us
    all_gather x1, waiting for transfers between devices, local(): scaled_all = lax.all_gather(scaled, 'blk', axis=0, tiled=True)  29.2 us
    all_gather x1, waiting for transfers between devices, local(): gathered = lax.all_gather(tokens, 'blk', axis=0, tiled=True)  21.7 us
    dot_general x3, matrix products, contract_cols(): lax.dot_general(left, right, (((1,), (1,)), ((), ())), preferred_element_...  20.2 us
    dot_general x3, matrix products, contract_rows(): lax.dot_general(left, right, (((0,), (0,)), ((), ())), preferred_element_...  19.6 us
  transfers between devices with their start and end apart: 7, of which 6 were waited for; matrix products, arithmetic and copies ran while one was open for 13% of the time, Pallas kernels for 0%

commit v1 on v0

--- a/solution.py
+++ b/solution.py
@@ -50,20 +50,14 @@
         scatter_dimension=0,
         tiled=True,
     )
-    term_gate = contract_rows(gathered, d_gate) * scales[0]
-    term_up = contract_rows(gathered, d_up) * scales[1]
-    term_down = contract_rows(hidden, scaled_all) * scales[2]
-    grad_gate, grad_up, grad_down = (
-        lax.psum_scatter(
-            term_gate.astype(jnp.bfloat16), "dp", scatter_dimension=0, tiled=True
-        ).astype(jnp.float32),
-        lax.psum_scatter(
-            term_up.astype(jnp.bfloat16), "dp", scatter_dimension=0, tiled=True
-        ).astype(jnp.float32),
-        lax.psum_scatter(
-            term_down.astype(jnp.bfloat16), "dp", scatter_dimension=1, tiled=True
-        ).astype(jnp.float32),
-    )
+    tokens_slice = lax.all_to_all(gathered, "dp", split_axis=1, concat_axis=0, tiled=True)
+    scaled_slice = lax.all_to_all(scaled_all, "dp", split_axis=1, concat_axis=0, tiled=True)
+    hidden_all = lax.all_gather(hidden, "dp", axis=0, tiled=True)
+    d_gate_all = lax.all_gather(d_gate, "dp", axis=0, tiled=True)
+    d_up_all = lax.all_gather(d_up, "dp", axis=0, tiled=True)
+    grad_gate = contract_rows(tokens_slice, d_gate_all) * scales[0]
+    grad_up = contract_rows(tokens_slice, d_up_all) * scales[1]
+    grad_down = contract_rows(hidden_all, scaled_slice) * scales[2]
     return (
         mixed,
         input_grad,

time: 384 us -> 318 us (0.83)
  waiting for transfers between devices: 299 us -> 225 us
  starting transfers between devices: 0.47 us -> 8.6 us
    reduce_scatter x3 -> x0, waiting for transfers between devices: 211 us -> none  [the longest x1 72.3 us: local(): lax.psum_scatter(term_down.astype(jnp.bfloat16), 'dp', scatter_dimension=...]
    all_gather x0 -> x3, waiting for transfers between devices: none -> 93.5 us  [the longest x1 34.6 us: local(): hidden_all = lax.all_gather(hidden, 'dp', axis=0, tiled=True)]
    reduce_scatter x1, waiting for transfers between devices: 0.02 us -> 31.9 us  [local(): lax.psum_scatter((jnp.dot(hidden, w_down, preferred_element_type=jnp.floa...]
    all_to_all x0 -> x2, waiting for transfers between devices: none -> 10.8 us  [the longest x1 10.8 us: local(): lax.all_to_all(gathered, 'dp', split_axis=1, concat_axis=0, tiled=True)]
    all_to_all x0 -> x2, starting transfers between devices: none -> 8.14 us  [the longest x1 4.55 us: local(): lax.all_to_all(gathered, 'dp', split_axis=1, concat_axis=0, tiled=True)]
    unnamed x20 -> x12, local copies, waits for them, and re-layouts: 8.98 us -> 4.79 us
  transfers between devices with their start and end apart: 7 -> 9, of which waited for: 6 -> 8; matrix products, arithmetic and copies ran while one was open for 13% -> 16% of each run, Pallas kernels for 0% -> 0%
where the time goes in v1:
time: 318 us; the launch traced here: 317 us
  waiting for transfers between devices  225 us (71%)
  matrix products  56 us (18%)
  between operations  14.2 us (4%)
  starting transfers between devices  8.6 us (3%)
  local copies, waits for them, and re-layouts  8.17 us (3%)
  other arithmetic  4.87 us (2%)
    reduce_scatter x1, waiting for transfers between devices, local(): lax.psum_scatter((contract_cols(d_gate, w_gate) * scales[0] + contract_co...  35.2 us
    all_gather x1, waiting for transfers between devices, local(): hidden_all = lax.all_gather(hidden, 'dp', axis=0, tiled=True)  34.6 us
    all_gather x1, waiting for transfers between devices, local(): d_up_all = lax.all_gather(d_up, 'dp', axis=0, tiled=True)  34 us
    reduce_scatter x1, waiting for transfers between devices, local(): lax.psum_scatter((jnp.dot(hidden, w_down, preferred_element_type=jnp.floa...  31.9 us
    all_gather x1, waiting for transfers between devices, local(): scaled_all = lax.all_gather(scaled, 'blk', axis=0, tiled=True)  29.2 us
    all_gather x1, waiting for transfers between devices, local(): d_gate_all = lax.all_gather(d_gate, 'dp', axis=0, tiled=True)  25 us
    all_gather x1, waiting for transfers between devices, local(): gathered = lax.all_gather(tokens, 'blk', axis=0, tiled=True)  22.9 us
    dot_general x3, matrix products, contract_cols(): lax.dot_general(left, right, (((1,), (1,)), ((), ())), preferred_element_...  18.9 us
  transfers between devices with their start and end apart: 9, of which 8 were waited for; matrix products, arithmetic and copies ran while one was open for 16% of the time, Pallas kernels for 0%

profile of v1, /device:TPU:0, one launch (start us, length us, event | category | flops | bytes accessed | tf_op | source)
XLA Modules:
  0.0 317.2 jit_solution(12840809473080515832)
XLA Ops:
  7.2 0.7 fusion.5
  7.9 1.7 multiply_convert_fusion.6
  9.7 0.7 all-gather.6.cloned.1.call-update
  10.5 0.7 multiply_exponential_fusion
  11.2 0.6 fusion.6
  11.8 29.2 %all-gather.8.cloned.1.call-done = bf16[320,3072]{1,0:T(8,128)(2,1)} async-done(((bf16[40,3072]{1,0:T(8,128)(2,1)}), bf16[320,3072]{1,0:T(8,128)(2,1)}) %all-gather.8.cloned.1.call-update) | async-done | bytes 1966096 | tf_op jit(solution)/shard_map/all_gather | solution.py:39
  41.0 6.3 %convolution_multiply_fusion.3 = f32[320,1024]{1,0:T(8,128)S(1)} fusion(bf16[320,3072]{1,0:T(8,128)(2,1)} %all-gather.8.cloned.1.call-done, bf16[1024,3072]{1,0:T(8,128)(2,1)} %param.14, f32[]{:T(128)} %bitcast.2), kind=kOutput, calls=%fused_computation.13 | convolution fusion | flops 2013593600 | bytes 9568260 | tf_op jit(solution)/shard_map/dot_general | solution.py:14
  47.2 22.9 %all-gather.6.cloned.1.call-done = bf16[320,3072]{1,0:T(8,128)(2,1)} async-done(((bf16[40,3072]{1,0:T(8,128)(2,1)}), bf16[320,3072]{1,0:T(8,128)(2,1)}) %all-gather.6.cloned.1.call-update) | async-done | bytes 1966096 | tf_op jit(solution)/shard_map/all_gather | solution.py:24
  70.2 6.3 %convolution_multiply_fusion.4 = f32[320,1024]{1,0:T(8,128)S(1)} fusion(bf16[320,3072]{1,0:T(8,128)(2,1)} %all-gather.6.cloned.1.call-done, bf16[3072,1024]{1,0:T(8,128)(2,1)} %param.13, f32[]{:T(128)} %bitcast.1), kind=kOutput, calls=%fused_computation.14 | convolution fusion | flops 2013593600 | bytes 9568260 | tf_op jit(solution)/shard_map/dot_general | solution.py:26
  76.4 7.5 %multiply_convert_fusion.4 = (bf16[320,1024]{1,0:T(8,128)(2,1)}, bf16[320,1024]{1,0:T(8,128)(2,1)}, bf16[320,1024]{1,0:T(8,128)(2,1)}) fusion(f32[320,1024]{1,0:T(8,128)S(1)} %convolution_multiply_fusion.3, f32[320,1024]{1,0:T(8,128)S(1)} %convolution_multiply_fusion.4, f32[]{:T(128)} %bitcast, bf16[320,3072]{1,0:T(8,128)(2,1)S(1)} %copy-done.1, ...), kind=kOutput, calls=%fused_computation.17 | convolution fusion | flops 2018836480 | bytes 12845060 | tf_op jit(solution)/shard_map/dot_general | solution.py:25
  84.1 0.5 all-gather.12.cloned.1.call-update
  84.6 0.5 all-gather.14.cloned.1.call-update
  85.2 7.0 %fusion.2 = bf16[320,3072]{1,0:T(8,128)(2,1)} fusion(bf16[320,1024]{1,0:T(8,128)(2,1)S(1)} %copy-done.2, bf16[1024,3072]{1,0:T(8,128)(2,1)} %param.14, f32[]{:T(128)} %bitcast.2), kind=kOutput, calls=%fused_computation.5 | convolution fusion | flops 2015232000 | bytes 8912900 | tf_op jit(solution)/shard_map/dot_general | solution.py:30
  92.3 1.4 copy.31
  93.7 4.5 %all-to-all-start = ((bf16[320,4,768]{2,0,1:T(8,128)(2,1)}), bf16[320,4,768]{2,0,1:T(8,128)(2,1)}, u32[]{:S(2)}, u32[]{:S(2)}) async-start(bf16[320,4,768]{2,0,1:T(8,128)(2,1)} %bitcast.38), calls=%async_computation.2 | async-start | bytes 3932160 | tf_op jit(solution)/shard_map/all_to_all | solution.py:53
  98.5 5.6 %convolution_multiply_fusion = f32[320,3072]{1,0:T(8,128)S(1)} fusion(bf16[320,1024]{1,0:T(8,128)(2,1)S(1)} %copy-done.3, bf16[3072,1024]{1,0:T(8,128)(2,1)} %param.13, f32[]{:T(128)} %bitcast.1), kind=kOutput, calls=%fused_computation | convolution fusion | flops 2014248960 | bytes 10878980 | tf_op jit(solution)/shard_map/dot_general | solution.py:14
  104.1 7.1 %fusion.1 = bf16[320,3072]{1,0:T(8,128)(2,1)} fusion(f32[320,3072]{1,0:T(8,128)S(1)} %convolution_multiply_fusion, bf16[320,1024]{1,0:T(8,128)(2,1)S(1)} %copy-done.4, bf16[3072,1024]{1,0:T(8,128)(2,1)} %param.12, f32[]{:T(128)} %bitcast), kind=kOutput, calls=%fused_computation.4 | convolution fusion | flops 2016215040 | bytes 12845060 | tf_op jit(solution)/shard_map/dot_general | solution.py:14
  111.2 1.5 copy-done
  112.7 1.4 copy.30
  114.1 10.8 %all-to-all-done = bf16[320,4,768]{2,0,1:T(8,128)(2,1)} async-done(((bf16[320,4,768]{2,0,1:T(8,128)(2,1)}), bf16[320,4,768]{2,0,1:T(8,128)(2,1)}, u32[]{:S(2)}, u32[]{:S(2)}) %all-to-all-start) | async-done | bytes 1966112 | tf_op jit(solution)/shard_map/all_to_all | solution.py:53
  124.9 3.6 %all-to-all-start.1 = ((bf16[320,4,768]{2,0,1:T(8,128)(2,1)}), bf16[320,4,768]{2,0,1:T(8,128)(2,1)S(1)}, u32[]{:S(2)}, u32[]{:S(2)}) async-start(bf16[320,4,768]{2,0,1:T(8,128)(2,1)} %bitcast.37), calls=%async_computation.3 | async-start | bytes 3932160 | tf_op jit(solution)/shard_map/all_to_all | solution.py:54
  128.5 25.0 %all-gather.10.cloned.1.call-done = bf16[1280,1024]{1,0:T(8,128)(2,1)} async-done(((bf16[320,1024]{1,0:T(8,128)(2,1)}), bf16[1280,1024]{1,0:T(8,128)(2,1)}) %all-gather.10.cloned.1.call-update) | async-done | bytes 2621456 | tf_op jit(solution)/shard_map/all_gather | solution.py:56
  153.5 5.3 %fusion.3 = bf16[768,1024]{0,1:T(8,128)(2,1)S(1)} fusion(f32[]{:T(128)} %bitcast, bf16[1280,1024]{1,0:T(8,128)(2,1)} %all-gather.10.cloned.1.call-done, bf16[1280,768]{1,0:T(8,128)(2,1)} %bitcast.4), kind=kOutput, calls=%fused_computation.11 | convolution fusion | flops 2014838784 | bytes 6160388 | tf_op jit(solution)/shard_map/dot_general | solution.py:8
  158.7 1.6 copy.24
  160.4 34.0 %all-gather.12.cloned.1.call-done = bf16[1280,1024]{1,0:T(8,128)(2,1)} async-done(((bf16[320,1024]{1,0:T(8,128)(2,1)}), bf16[1280,1024]{1,0:T(8,128)(2,1)}) %all-gather.12.cloned.1.call-update) | async-done | bytes 2621456 | tf_op jit(solution)/shard_map/all_gather | solution.py:57
  194.3 5.2 %fusion.4 = bf16[768,1024]{0,1:T(8,128)(2,1)S(1)} fusion(f32[]{:T(128)} %bitcast.1, bf16[1280,1024]{1,0:T(8,128)(2,1)} %all-gather.12.cloned.1.call-done, bf16[1280,768]{1,0:T(8,128)(2,1)} %bitcast.4), kind=kOutput, calls=%fused_computation.12 | convolution fusion | flops 2014838784 | bytes 6160388 | tf_op jit(solution)/shard_map/dot_general | solution.py:8
  199.5 1.6 copy.25
  201.1 34.6 %all-gather.14.cloned.1.call-done = bf16[1280,1024]{1,0:T(8,128)(2,1)} async-done(((bf16[320,1024]{1,0:T(8,128)(2,1)}), bf16[1280,1024]{1,0:T(8,128)(2,1)}) %all-gather.14.cloned.1.call-update) | async-done | bytes 2621456 | tf_op jit(solution)/shard_map/all_gather | solution.py:55
  235.7 5.8 %multiply_convert_fusion = bf16[1024,768]{1,0:T(8,128)(2,1)} fusion(bf16[1280,1024]{1,0:T(8,128)(2,1)} %all-gather.14.cloned.1.call-done, bf16[1280,768]{1,0:T(8,128)(2,1)S(1)} %bitcast.41, f32[]{:T(128)} %bitcast.2), kind=kOutput, calls=%fused_computation.6 | convolution fusion | flops 2014838784 | bytes 6160388 | tf_op jit(solution)/shard_map/dot_general | solution.py:8
  241.5 31.9 %reduce-scatter.3.cloned.1.call-done = bf16[40,3072]{1,0:T(8,128)(2,1)} async-done(((bf16[320,3072]{1,0:T(8,128)(2,1)}), bf16[40,3072]{1,0:T(8,128)(2,1)}) %reduce-scatter.3.cloned.1.call-update) | async-done | bytes 245776 | tf_op jit(solution)/shard_map/reduce_scatter | solution.py:29
  273.4 1.7 multiply_convert_fusion.7
  275.2 35.2 %reduce-scatter.5.cloned.1.call-done = bf16[40,3072]{1,0:T(8,128)(2,1)} async-done(((bf16[320,3072]{1,0:T(8,128)(2,1)}), bf16[40,3072]{1,0:T(8,128)(2,1)}) %reduce-scatter.5.cloned.1.call-update) | async-done | bytes 245776 | tf_op jit(solution)/shard_map/reduce_scatter | solution.py:45
  (21 shorter events, 0.5 us)
Async XLA Ops:
  7.2 33.8 %all-gather.8.cloned.1.call-start = ((), (), s32[]{:S(2)}) async-start(), calls=%async_computation.6 | async-start | bytes 2211840 | tf_op jit(solution)/shard_map/all_gather | solution.py:39
  9.7 60.5 %all-gather.6.cloned.1.call-start = ((), (), s32[]{:S(2)}) async-start(), calls=%async_computation.4 | async-start | bytes 2211840 | tf_op jit(solution)/shard_map/all_gather | solution.py:24
  10.4 143.0 %all-gather.10.cloned.1.call-start = ((), (), s32[]{:S(2)}) async-start(), calls=%async_computation.8 | async-start | bytes 3276800 | tf_op jit(solution)/shard_map/all_gather | solution.py:56
  70.2 6.3 %copy-start.1 = (bf16[320,3072]{1,0:T(8,128)(2,1)S(1)}, bf16[320,3072]{1,0:T(8,128)(2,1)}, u32[]{:S(2)}) copy-start(bf16[320,3072]{1,0:T(8,128)(2,1)} %all-gather.6.cloned.1.call-done) | copy-start | bytes 5898244
  84.0 1.2 copy-start.2
  84.0 110.3 %all-gather.12.cloned.1.call-start = ((), (), s32[]{:S(2)}) async-start(), calls=%async_computation.9 | async-start | bytes 3276800 | tf_op jit(solution)/shard_map/all_gather | solution.py:57
  84.6 151.1 %all-gather.14.cloned.1.call-start = ((), (), s32[]{:S(2)}) async-start(), calls=%async_computation.10 | async-start | bytes 3276800 | tf_op jit(solution)/shard_map/all_gather | solution.py:55
  85.2 188.2 %reduce-scatter.3.cloned.1.call-start = ((), (), s32[]{:S(2)}) async-start(), calls=%async_computation.5 | async-start | bytes 2211840 | tf_op jit(solution)/shard_map/reduce_scatter | solution.py:29
  93.7 4.8 %copy-start.3 = (bf16[320,1024]{1,0:T(8,128)(2,1)S(1)}, bf16[320,1024]{1,0:T(8,128)(2,1)}, u32[]{:S(2)}) copy-start(bf16[320,1024]{1,0:T(8,128)(2,1)} %get-tuple-element.27) | copy-start | bytes 1966084
  93.7 31.2 %all-to-all-start = ((bf16[320,4,768]{2,0,1:T(8,128)(2,1)}), bf16[320,4,768]{2,0,1:T(8,128)(2,1)}, u32[]{:S(2)}, u32[]{:S(2)}) async-start(bf16[320,4,768]{2,0,1:T(8,128)(2,1)} %bitcast.38), calls=%async_computation.2 | async-start | bytes 3932160 | tf_op jit(solution)/shard_map/all_to_all | solution.py:53
  98.2 5.8 %copy-start.4 = (bf16[320,1024]{1,0:T(8,128)(2,1)S(1)}, bf16[320,1024]{1,0:T(8,128)(2,1)}, u32[]{:S(2)}) copy-start(bf16[320,1024]{1,0:T(8,128)(2,1)} %get-tuple-element.25) | copy-start | bytes 1966084
  98.2 212.1 %reduce-scatter.5.cloned.1.call-start = ((), (), s32[]{:S(2)}) async-start(), calls=%async_computation.7 | async-start | bytes 2211840 | tf_op jit(solution)/shard_map/reduce_scatter | solution.py:45
  111.1 1.5 copy-start
  124.9 76.2 %all-to-all-start.1 = ((bf16[320,4,768]{2,0,1:T(8,128)(2,1)}), bf16[320,4,768]{2,0,1:T(8,128)(2,1)S(1)}, u32[]{:S(2)}, u32[]{:S(2)}) async-start(bf16[320,4,768]{2,0,1:T(8,128)(2,1)} %bitcast.37), calls=%async_computation.3 | async-start | bytes 3932160 | tf_op jit(solution)/shard_map/all_to_all | solution.py:54
Sparse Core Ops, SparseCore 0:
  10.2 30.7 all-gather.7
  42.6 27.5 all-gather.5
  84.1 69.2 all-gather.9
  155.7 38.5 all-gather.11
  196.0 39.6 all-gather.13
  237.9 35.4 reduce-scatter.2
  276.4 33.8 reduce-scatter.4

commit v2 on v1

v2 whole, which is shorter than its diff:
```python
import functools

import jax
import jax.numpy as jnp
from jax import lax
from jax.experimental import pallas as pl
from jax.experimental.pallas import tpu as pltpu
from jax.sharding import PartitionSpec as P


def contract_rows(left, right):
    return lax.dot_general(
        left, right, (((0,), (0,)), ((), ())), preferred_element_type=jnp.float32
    )


def contract_cols(left, right):
    return lax.dot_general(
        left, right, (((1,), (1,)), ((), ())), preferred_element_type=jnp.float32
    )


MESH = pl.DeviceIdType.MESH


def exchange_kernel(
    n, tok, sca, hid, dg, du, _out_part, _in_part, tok_o, sca_o, hid_o, dg_o, du_o, send, recv, fsend, frecv, own
):
    me = lax.axis_index("dp")
    blk = lax.axis_index("blk")
    core = blk % 2
    sibling = blk + 1 - 2 * core
    rows = hid.shape[0]
    half = rows // 2
    width = tok_o.shape[2]
    my_half = pl.ds(pl.multiple_of(core * half, 16), half)

    barrier = pltpu.get_barrier_semaphore()
    for j in range(1, n):
        pl.semaphore_signal(
            barrier, inc=1, device_id=((me + j) % n, blk), device_id_type=MESH
        )
    pl.semaphore_signal(barrier, inc=1, device_id=(me, sibling), device_id_type=MESH)
    pl.semaphore_wait(barrier, n)

    def columns(p):
        return pl.ds(pl.multiple_of(p * width, 128), width)

    slices = ((tok, tok_o), (sca, sca_o))
    wholes = ((hid, hid_o), (dg, dg_o), (du, du_o))
    sliced, sent, local = [], [], []
    for a, (src, dst) in enumerate(slices):
        for j in range(1, n):
            p = (me + j) % n
            copy = pltpu.make_async_remote_copy(
                src_ref=src.at[my_half, columns(p)],
                dst_ref=dst.at[me, my_half],
                send_sem=send.at[a, j],
                recv_sem=recv.at[a, j],
                device_id=(p, blk),
                device_id_type=MESH,
            )
            copy.start()
            sliced.append((a, j, dst, copy))
    for a, (src, dst) in enumerate(wholes):
        for j in range(1, n):
            p = (me + j) % n
            copy = pltpu.make_async_remote_copy(
                src_ref=src,
                dst_ref=dst.at[me],
                send_sem=send.at[2 + a, j],
                recv_sem=recv.at[2 + a, j],
                device_id=(p, blk),
                device_id_type=MESH,
            )
            copy.start()
            sent.append(copy)
    for a, (src, dst) in enumerate(slices):
        copy = pltpu.make_async_copy(src.at[:, columns(me)], dst.at[me], own.at[a])
        copy.start()
        local.append(copy)
    for a, (src, dst) in enumerate(wholes):
        copy = pltpu.make_async_copy(src, dst.at[me], own.at[2 + a])
        copy.start()
        local.append(copy)
    forwards = []
    for a, j, dst, copy in sliced:
        copy.wait_recv()
        landed = dst.at[(me + n - j) % n, my_half]
        forward = pltpu.make_async_remote_copy(
            src_ref=landed,
            dst_ref=landed,
            send_sem=fsend.at[a, j],
            recv_sem=frecv.at[a, j],
            device_id=(me, sibling),
            device_id_type=MESH,
        )
        forward.start()
        forwards.append(forward)
    for _, _, _, copy in sliced:
        copy.wait_send()
    for copy in forwards + sent + local:
        copy.wait()


def exchange(n, tokens, scaled, hidden, d_gate, d_up, out_part, in_part):
    rows, features = tokens.shape
    units = hidden.shape[1]
    part = jax.ShapeDtypeStruct((n, rows, features // n), jnp.bfloat16)
    whole = jax.ShapeDtypeStruct((n, rows, units), jnp.bfloat16)
    outs = pl.pallas_call(
        functools.partial(exchange_kernel, n),
        out_shape=(part, part, whole, whole, whole),
        in_specs=[pl.BlockSpec(memory_space=pl.ANY)] * 7,
        out_specs=[pl.BlockSpec(memory_space=pl.ANY)] * 5,
        scratch_shapes=[
            pltpu.SemaphoreType.DMA((5, n)),
            pltpu.SemaphoreType.DMA((5, n)),
            pltpu.SemaphoreType.DMA((2, n)),
            pltpu.SemaphoreType.DMA((2, n)),
            pltpu.SemaphoreType.DMA((5,)),
        ],
        compiler_params=pltpu.CompilerParams(collective_id=0, has_side_effects=True),
        cost_estimate=pl.CostEstimate(flops=0, bytes_accessed=300_000_000, transcendentals=0),
    )(tokens, scaled, hidden, d_gate, d_up, out_part, in_part)
    return [out.reshape(n * rows, out.shape[2]) for out in outs]


def local(n, tokens, expert_ids, route_probs, scale_exps, w_gate, w_up, w_down, out_grad):
    scales = jnp.exp2(scale_exps.astype(jnp.float32))
    combine = jnp.sum(jnp.where(expert_ids == 0, route_probs, jnp.zeros_like(route_probs)), axis=1)[
        :, None
    ]
    gathered = lax.all_gather(tokens, "blk", axis=0, tiled=True)
    gate_pre = jnp.dot(gathered, w_gate, preferred_element_type=jnp.float32) * scales[0]
    up_pre = jnp.dot(gathered, w_up, preferred_element_type=jnp.float32) * scales[1]
    sigmoid_gate = jax.nn.sigmoid(gate_pre)
    hidden = (gate_pre * sigmoid_gate * up_pre).astype(jnp.bfloat16)
    out_part = (jnp.dot(hidden, w_down, preferred_element_type=jnp.float32) * scales[2]).astype(
        jnp.bfloat16
    )
    scaled = (combine * out_grad.astype(jnp.float32)).astype(jnp.bfloat16)
    scaled_all = lax.all_gather(scaled, "blk", axis=0, tiled=True)
    d_hidden = contract_cols(scaled_all, w_down) * scales[2]
    d_gate = (d_hidden * up_pre * sigmoid_gate * (1.0 + gate_pre * (1.0 - sigmoid_gate))).astype(
        jnp.bfloat16
    )
    d_up = (d_hidden * gate_pre * sigmoid_gate).astype(jnp.bfloat16)
    in_part = (
        contract_cols(d_gate, w_gate) * scales[0] + contract_cols(d_up, w_up) * scales[1]
    ).astype(jnp.bfloat16)
    expert_out = lax.psum_scatter(out_part, "blk", scatter_dimension=0, tiled=True)
    mixed = (combine * expert_out.astype(jnp.float32)).astype(jnp.bfloat16)
    input_grad = lax.psum_scatter(in_part, "blk", scatter_dimension=0, tiled=True)
    tokens_slice, scaled_slice, hidden_all, d_gate_all, d_up_all = exchange(
        n, gathered, scaled_all, hidden, d_gate, d_up, out_part, in_part
    )
    grad_gate = contract_rows(tokens_slice, d_gate_all) * scales[0]
    grad_up = contract_rows(tokens_slice, d_up_all) * scales[1]
    grad_down = contract_rows(hidden_all, scaled_slice) * scales[2]
    return (
        mixed,
        input_grad,
        grad_gate.astype(jnp.bfloat16),
        grad_up.astype(jnp.bfloat16),
        grad_down.astype(jnp.bfloat16),
    )


def solution(mesh):
    return jax.shard_map(
        functools.partial(local, mesh.shape["dp"]),
        mesh=mesh,
        in_specs=(
            P(("dp", "blk"), None),
            P(("dp", "blk"), None),
            P(("dp", "blk"), None),
            P(),
            P(None, "blk"),
            P(None, "blk"),
            P("blk", None),
            P(("dp", "blk"), None),
        ),
        out_specs=(
            P(("dp", "blk"), None),
            P(("dp", "blk"), None),
            P("dp", "blk"),
            P("dp", "blk"),
            P("blk", "dp"),
        ),
        check_vma=False,
    )
```

time: 318 us -> 237 us (0.75)
  waiting for transfers between devices: 225 us -> 52.8 us
  Pallas kernels: 0 us -> 110 us
  starting transfers between devices: 8.6 us -> 0.34 us
  local copies, waits for them, and re-layouts: 8.17 us -> 1.54 us
  matrix products: 56 us -> 52.6 us
    pallas_call x0 -> x1, Pallas kernels: none -> 110 us  [exchange(): pl.pallas_call(functools.partial(exchange_kernel, n), out_shape=(part, pa...]
    all_gather x3 -> x0, waiting for transfers between devices: 93.5 us -> none  [the longest x1 34.6 us: local(): hidden_all = lax.all_gather(hidden, 'dp', axis=0, tiled=True)]
    reduce_scatter x2, waiting for transfers between devices: 67.1 us -> 0.01 us  [the longest x1 0.01 us: local(): lax.psum_scatter(out_part, 'blk', scatter_dimension=0, tiled=True)]
    all_to_all x2 -> x0, waiting for transfers between devices: 10.8 us -> none  [the longest x1 10.8 us: local(): lax.all_to_all(gathered, 'dp', split_axis=1, concat_axis=0, tiled=True)]
    all_to_all x2 -> x0, starting transfers between devices: 8.14 us -> none  [the longest x1 4.55 us: local(): lax.all_to_all(gathered, 'dp', split_axis=1, concat_axis=0, tiled=True)]
    unnamed x12 -> x20, local copies, waits for them, and re-layouts: 4.79 us -> 0.87 us
  transfers between devices with their start and end apart: 9 -> 4, of which waited for: 8 -> 2; matrix products, arithmetic and copies ran while one was open for 16% -> 16% of each run, Pallas kernels for 0% -> 47%
where the time goes in v2:
time: 237 us; the launch traced here: 236 us
  Pallas kernels  110 us (46%)
  waiting for transfers between devices  52.8 us (22%)
  matrix products  52.6 us (22%)
  between operations  13.9 us (6%)
  other arithmetic  4.87 us (2%)
    pallas_call x1, Pallas kernels, exchange(): pl.pallas_call(functools.partial(exchange_kernel, n), out_shape=(part, pa...  110 us
    all_gather x1, waiting for transfers between devices, local(): scaled_all = lax.all_gather(scaled, 'blk', axis=0, tiled=True)  29.1 us
    all_gather x1, waiting for transfers between devices, local(): gathered = lax.all_gather(tokens, 'blk', axis=0, tiled=True)  22.9 us
    dot_general x3, matrix products, contract_cols(): lax.dot_general(left, right, (((1,), (1,)), ((), ())), preferred_element_...  19 us
    dot_general x3, matrix products, contract_rows(): lax.dot_general(left, right, (((0,), (0,)), ((), ())), preferred_element_...  15.3 us
    dot_general x1, matrix products, local(): jnp.dot(gathered, w_gate, preferred_element_type=jnp.float32) * scales[0]  7.24 us
    dot_general x1, matrix products, local(): jnp.dot(gathered, w_up, preferred_element_type=jnp.float32) * scales[1]  6.8 us
  transfers between devices with their start and end apart: 4, of which 2 were waited for; matrix products, arithmetic and copies ran while one was open for 16% of the time, Pallas kernels for 47%

profile of v2, /device:TPU:0, one launch (start us, length us, event | category | flops | bytes accessed | tf_op | source)
XLA Modules:
  0.0 236.3 jit_solution(477054999951173561)
XLA Ops:
  7.2 0.0 all-gather.5.cloned.1.call-start
  7.2 0.7 fusion.6
  7.9 1.7 multiply_convert_fusion.3
  9.7 0.0 all-gather.5.cloned.1.call-update
  9.7 0.0 all-gather.3.cloned.1.call-start
  9.7 0.7 all-gather.3.cloned.1.call-update
  10.4 0.0 reduce-scatter.3.cloned.1.call-start
  10.5 0.7 multiply_exponential_fusion
  11.2 0.7 fusion.7
  11.8 29.1 %all-gather.5.cloned.1.call-done.sca = bf16[320,3072]{1,0:T(8,128)(2,1)} async-done(((bf16[40,3072]{1,0:T(8,128)(2,1)}), bf16[320,3072]{1,0:T(8,128)(2,1)}) %all-gather.5.cloned.1.call-update) | async-done | bytes 1966096 | tf_op jit(solution)/shard_map/all_gather | solution.py:143
  41.0 6.3 %convolution_multiply_fusion.3 = f32[320,1024]{1,0:T(8,128)S(1)} fusion(bf16[320,3072]{1,0:T(8,128)(2,1)} %all-gather.5.cloned.1.call-done.sca, bf16[1024,3072]{1,0:T(8,128)(2,1)} %param.14, f32[]{:T(128)} %bitcast.2), kind=kOutput, calls=%fused_computation.12 | convolution fusion | flops 2013593600 | bytes 9568260 | tf_op jit(solution)/shard_map/dot_general | solution.py:18
  47.2 22.9 %all-gather.3.cloned.1.call-done.tok = bf16[320,3072]{1,0:T(8,128)(2,1)} async-done(((bf16[40,3072]{1,0:T(8,128)(2,1)}), bf16[320,3072]{1,0:T(8,128)(2,1)}) %all-gather.3.cloned.1.call-update) | async-done | bytes 1966096 | tf_op jit(solution)/shard_map/all_gather | solution.py:134
  70.2 6.8 %convolution_multiply_fusion.4 = f32[320,1024]{1,0:T(8,128)S(1)} fusion(bf16[320,3072]{1,0:T(8,128)(2,1)} %all-gather.3.cloned.1.call-done.tok, bf16[3072,1024]{1,0:T(8,128)(2,1)} %param.13, f32[]{:T(128)} %bitcast.1), kind=kOutput, calls=%fused_computation.13 | convolution fusion | flops 2013593600 | bytes 9568260 | tf_op jit(solution)/shard_map/dot_general | solution.py:136
  77.0 0.0 copy-done
  77.0 0.0 slice-start.1
  77.0 7.2 %multiply_convert_fusion.1 = (bf16[320,1024]{1,0:T(8,128)(2,1)S(1)}, bf16[320,1024]{1,0:T(8,128)(2,1)S(1)}, bf16[320,1024]{1,0:T(8,128)(2,1)}) fusion(f32[320,1024]{1,0:T(8,128)S(1)} %convolution_multiply_fusion.3, f32[320,1024]{1,0:T(8,128)S(1)} %convolution_multiply_fusion.4, f32[]{:T(128)} %bitcast, bf16[320,3072]{1,0:T(8,128)(2,1)S(1)} %copy-done, ...), kind=kOutput, calls=%fused_computation.16 | convolution fusion | flops 2018836480 | bytes 12845060 | tf_op jit(solution)/shard_map/dot_general | solution.py:135
  84.2 0.0 slice-done
  84.2 0.0 slice-done.1
  84.3 4.3 %fusion.2._out_part = bf16[320,3072]{1,0:T(8,128)(2,1)} fusion(bf16[320,1024]{1,0:T(8,128)(2,1)S(1)} %get-tuple-element.16.hid, bf16[1024,3072]{1,0:T(8,128)(2,1)S(1)} %bitcast.34, f32[]{:T(128)} %bitcast.2), kind=kOutput, calls=%fused_computation.5 | convolution fusion | flops 2015232000 | bytes 8912900 | tf_op jit(solution)/shard_map/dot_general | solution.py:139
  88.5 0.0 copy-done.2
  88.6 0.0 reduce-scatter.3.cloned.1.call-update
  88.6 0.2 reduce-scatter.5.cloned.1.call-start
  88.8 0.8 copy-done.3
  89.6 5.7 %convolution_multiply_fusion = f32[320,3072]{1,0:T(8,128)S(1)} fusion(bf16[320,1024]{1,0:T(8,128)(2,1)S(1)} %copy-done.3, bf16[3072,1024]{1,0:T(8,128)(2,1)} %param.13, f32[]{:T(128)} %bitcast.1), kind=kOutput, calls=%fused_computation | convolution fusion | flops 2014248960 | bytes 10878980 | tf_op jit(solution)/shard_map/dot_general | solution.py:18
  95.4 0.0 copy-done.1
  95.4 7.0 %fusion.1._in_part = bf16[320,3072]{1,0:T(8,128)(2,1)} fusion(f32[320,3072]{1,0:T(8,128)S(1)} %convolution_multiply_fusion, bf16[320,1024]{1,0:T(8,128)(2,1)S(1)} %get-tuple-element.15.dg, bf16[3072,1024]{1,0:T(8,128)(2,1)} %param.12, f32[]{:T(128)} %bitcast), kind=kOutput, calls=%fused_computation.4 | convolution fusion | flops 2016215040 | bytes 12845060 | tf_op jit(solution)/shard_map/dot_general | solution.py:18
  102.4 0.0 reduce-scatter.5.cloned.1.call-update
  102.4 110.3 %shard_map.119 = (bf16[4,320,768]{2,1,0:T(8,128)(2,1)}, bf16[4,320,768]{2,1,0:T(8,128)(2,1)}, bf16[4,320,1024]{2,1,0:T(8,128)(2,1)}, bf16[4,320,1024]{2,1,0:T(8,128)(2,1)}, bf16[4,320,1024]{2,1,0:T(8,128)(2,1)}) custom-call(bf16[320,3072]{1,0:T(8,128)(2,1)} %all-gather.3.cloned.1.call-done.tok, bf16[320,3072]{1,0:T(8,128)(2,1)} %all-gather.5.cloned.1.call-done.sca, ...), custom_call_target="tpu_custom_call" | custom-call | bytes 300000000 | tf_op jit(solution)/shard_map/pallas_call | solution.py:111
  212.7 7.0 %fusion.4 = bf16[768,1024]{1,0:T(8,128)(2,1)} fusion(bf16[4,320,768]{2,1,0:T(8,128)(2,1)} %get-tuple-element.10, bf16[4,320,1024]{2,1,0:T(8,128)(2,1)} %get-tuple-element.12, f32[]{:T(128)} %bitcast.1), kind=kOutput, calls=%fused_computation.9 | convolution fusion | flops 2014838784 | bytes 6160388 | tf_op jit(solution)/shard_map/dot_general | solution.py:12
  219.7 4.2 %fusion.5 = bf16[768,1024]{1,0:T(8,128)(2,1)} fusion(bf16[4,320,768]{2,1,0:T(8,128)(2,1)S(1)} %copy-done.7, bf16[4,320,1024]{2,1,0:T(8,128)(2,1)S(1)} %copy-done.5, f32[]{:T(128)} %bitcast), kind=kOutput, calls=%fused_computation.11 | convolution fusion | flops 2014838784 | bytes 6160388 | tf_op jit(solution)/shard_map/dot_general | solution.py:12
  223.9 4.2 %fusion.3 = bf16[1024,768]{1,0:T(8,128)(2,1)} fusion(bf16[4,320,1024]{2,1,0:T(8,128)(2,1)S(1)} %copy-done.4, bf16[4,320,768]{2,1,0:T(8,128)(2,1)S(1)} %copy-done.6, f32[]{:T(128)} %bitcast.2), kind=kOutput, calls=%fused_computation.7 | convolution fusion | flops 2014838784 | bytes 6160388 | tf_op jit(solution)/shard_map/dot_general | solution.py:12
  228.0 1.7 multiply_convert_fusion.4
  (16 shorter events, 0.0 us)
Async XLA Ops:
  7.2 33.8 %all-gather.5.cloned.1.call-start = ((), (), s32[]{:S(2)}) async-start(), calls=%async_computation.4 | async-start | bytes 2211840 | tf_op jit(solution)/shard_map/all_gather | solution.py:143
  9.7 60.5 %all-gather.3.cloned.1.call-start = ((), (), s32[]{:S(2)}) async-start(), calls=%async_computation.2 | async-start | bytes 2211840 | tf_op jit(solution)/shard_map/all_gather | solution.py:134
  10.4 217.6 %reduce-scatter.3.cloned.1.call-start = ((), (), s32[]{:S(2)}) async-start(), calls=%async_computation.3 | async-start | bytes 2211840 | tf_op jit(solution)/shard_map/reduce_scatter | solution.py:152
  70.2 6.8 %copy-start = (bf16[320,3072]{1,0:T(8,128)(2,1)S(1)}, bf16[320,3072]{1,0:T(8,128)(2,1)}, u32[]{:S(2)}) copy-start(bf16[320,3072]{1,0:T(8,128)(2,1)} %all-gather.3.cloned.1.call-done.tok) | copy-start | bytes 5898244
  70.2 14.1 %slice-start = ((s8[6291456]{0:T(1024)(128)(4,1)}), s8[4194304]{0:T(1024)(128)(4,1)S(1)}, s32[]{:S(2)}) async-start(s8[6291456]{0:T(1024)(128)(4,1)} %bitcast.33), calls=%async_computation.6 | async-start | bytes 8388608
  77.0 7.3 %slice-start.1 = ((s8[6291456]{0:T(1024)(128)(4,1)}), s8[2097152]{0:T(1024)(128)(4,1)S(1)}, s32[]{:S(2)}) async-start(s8[6291456]{0:T(1024)(128)(4,1)} %bitcast.33), calls=%async_computation.7 | async-start | bytes 4194304
  84.2 4.3 %copy-start.2 = (bf16[320,1024]{1,0:T(8,128)(2,1)}, bf16[320,1024]{1,0:T(8,128)(2,1)S(1)}, u32[]{:S(2)}) copy-start(bf16[320,1024]{1,0:T(8,128)(2,1)S(1)} %get-tuple-element.16.hid) | copy-start | bytes 1966084
  84.2 11.1 %copy-start.1 = (bf16[320,1024]{1,0:T(8,128)(2,1)}, bf16[320,1024]{1,0:T(8,128)(2,1)S(1)}, u32[]{:S(2)}) copy-start(bf16[320,1024]{1,0:T(8,128)(2,1)S(1)} %get-tuple-element.15.dg) | copy-start | bytes 1966084
  88.6 1.1 copy-start.3
  88.6 141.2 %reduce-scatter.5.cloned.1.call-start = ((), (), s32[]{:S(2)}) async-start(), calls=%async_computation.5 | async-start | bytes 2211840 | tf_op jit(solution)/shard_map/reduce_scatter | solution.py:154
  212.7 7.0 %copy-start.5 = (bf16[4,320,1024]{2,1,0:T(8,128)(2,1)S(1)}, bf16[4,320,1024]{2,1,0:T(8,128)(2,1)}, u32[]{:S(2)}) copy-start(bf16[4,320,1024]{2,1,0:T(8,128)(2,1)} %get-tuple-element.11) | copy-start | bytes 7864324
  212.7 7.0 %copy-start.7 = (bf16[4,320,768]{2,1,0:T(8,128)(2,1)S(1)}, bf16[4,320,768]{2,1,0:T(8,128)(2,1)}, u32[]{:S(2)}) copy-start(bf16[4,320,768]{2,1,0:T(8,128)(2,1)} %get-tuple-element.10) | copy-start | bytes 5898244
  219.7 4.2 %copy-start.4 = (bf16[4,320,1024]{2,1,0:T(8,128)(2,1)S(1)}, bf16[4,320,1024]{2,1,0:T(8,128)(2,1)}, u32[]{:S(2)}) copy-start(bf16[4,320,1024]{2,1,0:T(8,128)(2,1)} %get-tuple-element.13) | copy-start | bytes 7864324
  219.7 4.2 %copy-start.6 = (bf16[4,320,768]{2,1,0:T(8,128)(2,1)S(1)}, bf16[4,320,768]{2,1,0:T(8,128)(2,1)}, u32[]{:S(2)}) copy-start(bf16[4,320,768]{2,1,0:T(8,128)(2,1)} %get-tuple-element.14) | copy-start | bytes 5898244
Sparse Core Ops, SparseCore 0:
  10.2 30.7 all-gather.4
  42.6 27.5 all-gather.2
  88.7 34.9 reduce-scatter.2
  126.6 33.6 reduce-scatter.4

commit v3 on v2

--- a/solution.py
+++ b/solution.py
@@ -62,9 +62,13 @@
             )
             copy.start()
             sliced.append((a, j, dst, copy))
+    across, along = me + 1 - 2 * (me % 2), (me + 2) % n
+    passed = []
     for a, (src, dst) in enumerate(wholes):
-        for j in range(1, n):
+        for j in range(1, 3 if n == 4 else n):
             p = (me + j) % n
+            if n == 4:
+                p = across if j == 1 else along
             copy = pltpu.make_async_remote_copy(
                 src_ref=src,
                 dst_ref=dst.at[me],
@@ -74,7 +78,7 @@
                 device_id_type=MESH,
             )
             copy.start()
-            sent.append(copy)
+            (passed if n == 4 else sent).append((a, j, dst, copy))
     for a, (src, dst) in enumerate(slices):
         copy = pltpu.make_async_copy(src.at[:, columns(me)], dst.at[me], own.at[a])
         copy.start()
@@ -97,9 +101,23 @@
         )
         forward.start()
         forwards.append(forward)
-    for _, _, _, copy in sliced:
+    for a, j, dst, copy in passed:
+        copy.wait_recv()
+        owner, target = (across, along) if j == 1 else (along, across)
+        landed = dst.at[owner, pl.ds((j - 1) * half, half)]
+        forward = pltpu.make_async_remote_copy(
+            src_ref=landed,
+            dst_ref=landed,
+            send_sem=fsend.at[2 + a, j],
+            recv_sem=frecv.at[2 + a, j],
+            device_id=(target, blk),
+            device_id_type=MESH,
+        )
+        forward.start()
+        forwards.append(forward)
+    for _, _, _, copy in sliced + passed:
         copy.wait_send()
-    for copy in forwards + sent + local:
+    for copy in forwards + [copy for _, _, _, copy in sent] + local:
         copy.wait()
 
 
@@ -116,8 +134,8 @@
         scratch_shapes=[
             pltpu.SemaphoreType.DMA((5, n)),
             pltpu.SemaphoreType.DMA((5, n)),
-            pltpu.SemaphoreType.DMA((2, n)),
-            pltpu.SemaphoreType.DMA((2, n)),
+            pltpu.SemaphoreType.DMA((5, n)),
+            pltpu.SemaphoreType.DMA((5, n)),
             pltpu.SemaphoreType.DMA((5,)),
         ],
         compiler_params=pltpu.CompilerParams(collective_id=0, has_side_effects=True),

time: 237 us -> 220 us (0.928)
  Pallas kernels: 110 us -> 93.6 us
    pallas_call x1, Pallas kernels: 110 us -> 93.6 us  [exchange(): pl.pallas_call(functools.partial(exchange_kernel, n), out_shape=(part, pa...]
  transfers between devices with their start and end apart: 4 -> 4, of which waited for: 2 -> 2; matrix products, arithmetic and copies ran while one was open for 16% -> 17% of each run, Pallas kernels for 47% -> 43%
where the time goes in v3:
time: 220 us
  Pallas kernels  93.6 us (43%)
  waiting for transfers between devices  52.8 us (24%)
  matrix products  52.6 us (24%)
  between operations  13.9 us (6%)
  other arithmetic  4.87 us (2%)
    pallas_call x1, Pallas kernels, exchange(): pl.pallas_call(functools.partial(exchange_kernel, n), out_shape=(part, pa...  93.6 us
    all_gather x1, waiting for transfers between devices, local(): scaled_all = lax.all_gather(scaled, 'blk', axis=0, tiled=True)  29.1 us
    all_gather x1, waiting for transfers between devices, local(): gathered = lax.all_gather(tokens, 'blk', axis=0, tiled=True)  22.9 us
    dot_general x3, matrix products, contract_cols(): lax.dot_general(left, right, (((1,), (1,)), ((), ())), preferred_element_...  19 us
    dot_general x3, matrix products, contract_rows(): lax.dot_general(left, right, (((0,), (0,)), ((), ())), preferred_element_...  15.3 us
    dot_general x1, matrix products, local(): jnp.dot(gathered, w_gate, preferred_element_type=jnp.float32) * scales[0]  7.24 us
    dot_general x1, matrix products, local(): jnp.dot(gathered, w_up, preferred_element_type=jnp.float32) * scales[1]  6.8 us
  transfers between devices with their start and end apart: 4, of which 2 were waited for; matrix products, arithmetic and copies ran while one was open for 17% of the time, Pallas kernels for 43%

profile of v3, /device:TPU:0, one launch (start us, length us, event | category | flops | bytes accessed | tf_op | source)
XLA Modules:
  0.0 219.7 jit_solution(15198167929555145586)
XLA Ops:
  7.2 0.0 all-gather.5.cloned.1.call-start
  7.2 0.7 fusion.6
  7.9 1.7 multiply_convert_fusion.3
  9.7 0.0 all-gather.5.cloned.1.call-update
  9.7 0.0 all-gather.3.cloned.1.call-start
  9.7 0.7 all-gather.3.cloned.1.call-update
  10.4 0.0 reduce-scatter.3.cloned.1.call-start
  10.5 0.7 multiply_exponential_fusion
  11.2 0.7 fusion.7
  11.8 29.1 %all-gather.5.cloned.1.call-done.sca = bf16[320,3072]{1,0:T(8,128)(2,1)} async-done(((bf16[40,3072]{1,0:T(8,128)(2,1)}), bf16[320,3072]{1,0:T(8,128)(2,1)}) %all-gather.5.cloned.1.call-update) | async-done | bytes 1966096 | tf_op jit(solution)/shard_map/all_gather | solution.py:161
  41.0 6.3 %convolution_multiply_fusion.3 = f32[320,1024]{1,0:T(8,128)S(1)} fusion(bf16[320,3072]{1,0:T(8,128)(2,1)} %all-gather.5.cloned.1.call-done.sca, bf16[1024,3072]{1,0:T(8,128)(2,1)} %param.14, f32[]{:T(128)} %bitcast.2), kind=kOutput, calls=%fused_computation.12 | convolution fusion | flops 2013593600 | bytes 9568260 | tf_op jit(solution)/shard_map/dot_general | solution.py:18
  47.2 22.9 %all-gather.3.cloned.1.call-done.tok = bf16[320,3072]{1,0:T(8,128)(2,1)} async-done(((bf16[40,3072]{1,0:T(8,128)(2,1)}), bf16[320,3072]{1,0:T(8,128)(2,1)}) %all-gather.3.cloned.1.call-update) | async-done | bytes 1966096 | tf_op jit(solution)/shard_map/all_gather | solution.py:152
  70.2 6.8 %convolution_multiply_fusion.4 = f32[320,1024]{1,0:T(8,128)S(1)} fusion(bf16[320,3072]{1,0:T(8,128)(2,1)} %all-gather.3.cloned.1.call-done.tok, bf16[3072,1024]{1,0:T(8,128)(2,1)} %param.13, f32[]{:T(128)} %bitcast.1), kind=kOutput, calls=%fused_computation.13 | convolution fusion | flops 2013593600 | bytes 9568260 | tf_op jit(solution)/shard_map/dot_general | solution.py:154
  77.0 0.0 slice-start.1
  77.0 7.2 %multiply_convert_fusion.1 = (bf16[320,1024]{1,0:T(8,128)(2,1)S(1)}, bf16[320,1024]{1,0:T(8,128)(2,1)S(1)}, bf16[320,1024]{1,0:T(8,128)(2,1)}) fusion(f32[320,1024]{1,0:T(8,128)S(1)} %convolution_multiply_fusion.3, f32[320,1024]{1,0:T(8,128)S(1)} %convolution_multiply_fusion.4, f32[]{:T(128)} %bitcast, bf16[320,3072]{1,0:T(8,128)(2,1)S(1)} %copy-done, ...), kind=kOutput, calls=%fused_computation.16 | convolution fusion | flops 2018836480 | bytes 12845060 | tf_op jit(solution)/shard_map/dot_general | solution.py:153
  84.3 4.3 %fusion.2._out_part = bf16[320,3072]{1,0:T(8,128)(2,1)} fusion(bf16[320,1024]{1,0:T(8,128)(2,1)S(1)} %get-tuple-element.16.hid, bf16[1024,3072]{1,0:T(8,128)(2,1)S(1)} %bitcast.34, f32[]{:T(128)} %bitcast.2), kind=kOutput, calls=%fused_computation.5 | convolution fusion | flops 2015232000 | bytes 8912900 | tf_op jit(solution)/shard_map/dot_general | solution.py:157
  88.6 0.0 reduce-scatter.3.cloned.1.call-update
  88.6 0.2 reduce-scatter.5.cloned.1.call-start
  88.8 0.8 copy-done.3
  89.6 5.7 %convolution_multiply_fusion = f32[320,3072]{1,0:T(8,128)S(1)} fusion(bf16[320,1024]{1,0:T(8,128)(2,1)S(1)} %copy-done.3, bf16[3072,1024]{1,0:T(8,128)(2,1)} %param.13, f32[]{:T(128)} %bitcast.1), kind=kOutput, calls=%fused_computation | convolution fusion | flops 2014248960 | bytes 10878980 | tf_op jit(solution)/shard_map/dot_general | solution.py:18
  95.4 0.0 copy-done.1
  95.4 7.0 %fusion.1._in_part = bf16[320,3072]{1,0:T(8,128)(2,1)} fusion(f32[320,3072]{1,0:T(8,128)S(1)} %convolution_multiply_fusion, bf16[320,1024]{1,0:T(8,128)(2,1)S(1)} %get-tuple-element.15.dg, bf16[3072,1024]{1,0:T(8,128)(2,1)} %param.12, f32[]{:T(128)} %bitcast), kind=kOutput, calls=%fused_computation.4 | convolution fusion | flops 2016215040 | bytes 12845060 | tf_op jit(solution)/shard_map/dot_general | solution.py:18
  102.4 0.0 reduce-scatter.5.cloned.1.call-update
  102.4 93.6 %shard_map.119 = (bf16[4,320,768]{2,1,0:T(8,128)(2,1)}, bf16[4,320,768]{2,1,0:T(8,128)(2,1)}, bf16[4,320,1024]{2,1,0:T(8,128)(2,1)}, bf16[4,320,1024]{2,1,0:T(8,128)(2,1)}, bf16[4,320,1024]{2,1,0:T(8,128)(2,1)}) custom-call(bf16[320,3072]{1,0:T(8,128)(2,1)} %all-gather.3.cloned.1.call-done.tok, bf16[320,3072]{1,0:T(8,128)(2,1)} %all-gather.5.cloned.1.call-done.sca, ...), custom_call_target="tpu_custom_call" | custom-call | bytes 300000000 | tf_op jit(solution)/shard_map/pallas_call | solution.py:129
  196.0 0.0 copy-start.5
  196.0 0.0 copy-start.7
  196.0 7.0 %fusion.4 = bf16[768,1024]{1,0:T(8,128)(2,1)} fusion(bf16[4,320,768]{2,1,0:T(8,128)(2,1)} %get-tuple-element.10, bf16[4,320,1024]{2,1,0:T(8,128)(2,1)} %get-tuple-element.12, f32[]{:T(128)} %bitcast.1), kind=kOutput, calls=%fused_computation.9 | convolution fusion | flops 2014838784 | bytes 6160388 | tf_op jit(solution)/shard_map/dot_general | solution.py:12
  203.0 0.0 copy-done.7
  203.0 4.2 %fusion.5 = bf16[768,1024]{1,0:T(8,128)(2,1)} fusion(bf16[4,320,768]{2,1,0:T(8,128)(2,1)S(1)} %copy-done.7, bf16[4,320,1024]{2,1,0:T(8,128)(2,1)S(1)} %copy-done.5, f32[]{:T(128)} %bitcast), kind=kOutput, calls=%fused_computation.11 | convolution fusion | flops 2014838784 | bytes 6160388 | tf_op jit(solution)/shard_map/dot_general | solution.py:12
  207.2 0.0 copy-done.4
  207.2 4.2 %fusion.3 = bf16[1024,768]{1,0:T(8,128)(2,1)} fusion(bf16[4,320,1024]{2,1,0:T(8,128)(2,1)S(1)} %copy-done.4, bf16[4,320,768]{2,1,0:T(8,128)(2,1)S(1)} %copy-done.6, f32[]{:T(128)} %bitcast.2), kind=kOutput, calls=%fused_computation.7 | convolution fusion | flops 2014838784 | bytes 6160388 | tf_op jit(solution)/shard_map/dot_general | solution.py:12
  211.4 1.7 multiply_convert_fusion.4
  (16 shorter events, 0.0 us)
Async XLA Ops:
  7.2 33.8 %all-gather.5.cloned.1.call-start = ((), (), s32[]{:S(2)}) async-start(), calls=%async_computation.4 | async-start | bytes 2211840 | tf_op jit(solution)/shard_map/all_gather | solution.py:161
  9.7 60.5 %all-gather.3.cloned.1.call-start = ((), (), s32[]{:S(2)}) async-start(), calls=%async_computation.2 | async-start | bytes 2211840 | tf_op jit(solution)/shard_map/all_gather | solution.py:152
  10.4 200.9 %reduce-scatter.3.cloned.1.call-start = ((), (), s32[]{:S(2)}) async-start(), calls=%async_computation.3 | async-start | bytes 2211840 | tf_op jit(solution)/shard_map/reduce_scatter | solution.py:170
  70.2 6.8 %copy-start = (bf16[320,3072]{1,0:T(8,128)(2,1)S(1)}, bf16[320,3072]{1,0:T(8,128)(2,1)}, u32[]{:S(2)}) copy-start(bf16[320,3072]{1,0:T(8,128)(2,1)} %all-gather.3.cloned.1.call-done.tok) | copy-start | bytes 5898244
  70.2 14.1 %slice-start = ((s8[6291456]{0:T(1024)(128)(4,1)}), s8[4194304]{0:T(1024)(128)(4,1)S(1)}, s32[]{:S(2)}) async-start(s8[6291456]{0:T(1024)(128)(4,1)} %bitcast.33), calls=%async_computation.6 | async-start | bytes 8388608
  77.0 7.3 %slice-start.1 = ((s8[6291456]{0:T(1024)(128)(4,1)}), s8[2097152]{0:T(1024)(128)(4,1)S(1)}, s32[]{:S(2)}) async-start(s8[6291456]{0:T(1024)(128)(4,1)} %bitcast.33), calls=%async_computation.7 | async-start | bytes 4194304
  84.2 4.3 %copy-start.2 = (bf16[320,1024]{1,0:T(8,128)(2,1)}, bf16[320,1024]{1,0:T(8,128)(2,1)S(1)}, u32[]{:S(2)}) copy-start(bf16[320,1024]{1,0:T(8,128)(2,1)S(1)} %get-tuple-element.16.hid) | copy-start | bytes 1966084
  84.2 11.1 %copy-start.1 = (bf16[320,1024]{1,0:T(8,128)(2,1)}, bf16[320,1024]{1,0:T(8,128)(2,1)S(1)}, u32[]{:S(2)}) copy-start(bf16[320,1024]{1,0:T(8,128)(2,1)S(1)} %get-tuple-element.15.dg) | copy-start | bytes 1966084
  88.6 1.1 copy-start.3
  88.6 124.6 %reduce-scatter.5.cloned.1.call-start = ((), (), s32[]{:S(2)}) async-start(), calls=%async_computation.5 | async-start | bytes 2211840 | tf_op jit(solution)/shard_map/reduce_scatter | solution.py:172
  196.0 7.0 %copy-start.5 = (bf16[4,320,1024]{2,1,0:T(8,128)(2,1)S(1)}, bf16[4,320,1024]{2,1,0:T(8,128)(2,1)}, u32[]{:S(2)}) copy-start(bf16[4,320,1024]{2,1,0:T(8,128)(2,1)} %get-tuple-element.11) | copy-start | bytes 7864324
  196.0 7.0 %copy-start.7 = (bf16[4,320,768]{2,1,0:T(8,128)(2,1)S(1)}, bf16[4,320,768]{2,1,0:T(8,128)(2,1)}, u32[]{:S(2)}) copy-start(bf16[4,320,768]{2,1,0:T(8,128)(2,1)} %get-tuple-element.10) | copy-start | bytes 5898244
  203.0 4.2 %copy-start.4 = (bf16[4,320,1024]{2,1,0:T(8,128)(2,1)S(1)}, bf16[4,320,1024]{2,1,0:T(8,128)(2,1)}, u32[]{:S(2)}) copy-start(bf16[4,320,1024]{2,1,0:T(8,128)(2,1)} %get-tuple-element.13) | copy-start | bytes 7864324
  203.0 4.2 %copy-start.6 = (bf16[4,320,768]{2,1,0:T(8,128)(2,1)S(1)}, bf16[4,320,768]{2,1,0:T(8,128)(2,1)}, u32[]{:S(2)}) copy-start(bf16[4,320,768]{2,1,0:T(8,128)(2,1)} %get-tuple-element.14) | copy-start | bytes 5898244
Sparse Core Ops, SparseCore 0:
  10.2 30.7 all-gather.4
  42.6 27.5 all-gather.2
  88.7 34.9 reduce-scatter.2
  126.6 33.7 reduce-scatter.4

commit v4 on v3

--- a/solution.py
+++ b/solution.py
@@ -23,16 +23,19 @@
 MESH = pl.DeviceIdType.MESH
 
 
-def exchange_kernel(
-    n, tok, sca, hid, dg, du, _out_part, _in_part, tok_o, sca_o, hid_o, dg_o, du_o, send, recv, fsend, frecv, own
-):
+def exchange_kernel(n, n_slices, n_wholes, n_order, *refs):
+    total = n_slices + n_wholes
+    ins, outs = refs[:total], refs[total + n_order : 2 * total + n_order]
+    send, recv, fsend, frecv, own = refs[-5:]
+    slices = tuple(zip(ins[:n_slices], outs[:n_slices]))
+    wholes = tuple(zip(ins[n_slices:], outs[n_slices:]))
     me = lax.axis_index("dp")
     blk = lax.axis_index("blk")
     core = blk % 2
     sibling = blk + 1 - 2 * core
-    rows = hid.shape[0]
+    rows = ins[0].shape[0]
     half = rows // 2
-    width = tok_o.shape[2]
+    width = outs[0].shape[2]
     my_half = pl.ds(pl.multiple_of(core * half, 16), half)
 
     barrier = pltpu.get_barrier_semaphore()
@@ -46,8 +49,6 @@
     def columns(p):
         return pl.ds(pl.multiple_of(p * width, 128), width)
 
-    slices = ((tok, tok_o), (sca, sca_o))
-    wholes = ((hid, hid_o), (dg, dg_o), (du, du_o))
     sliced, sent, local = [], [], []
     for a, (src, dst) in enumerate(slices):
         for j in range(1, n):
@@ -72,8 +73,8 @@
             copy = pltpu.make_async_remote_copy(
                 src_ref=src,
                 dst_ref=dst.at[me],
-                send_sem=send.at[2 + a, j],
-                recv_sem=recv.at[2 + a, j],
+                send_sem=send.at[n_slices + a, j],
+                recv_sem=recv.at[n_slices + a, j],
                 device_id=(p, blk),
                 device_id_type=MESH,
             )
@@ -84,7 +85,7 @@
         copy.start()
         local.append(copy)
     for a, (src, dst) in enumerate(wholes):
-        copy = pltpu.make_async_copy(src, dst.at[me], own.at[2 + a])
+        copy = pltpu.make_async_copy(src, dst.at[me], own.at[n_slices + a])
         copy.start()
         local.append(copy)
     forwards = []
@@ -108,8 +109,8 @@
         forward = pltpu.make_async_remote_copy(
             src_ref=landed,
             dst_ref=landed,
-            send_sem=fsend.at[2 + a, j],
-            recv_sem=frecv.at[2 + a, j],
+            send_sem=fsend.at[n_slices + a, j],
+            recv_sem=frecv.at[n_slices + a, j],
             device_id=(target, blk),
             device_id_type=MESH,
         )
@@ -121,27 +122,27 @@
         copy.wait()
 
 
-def exchange(n, tokens, scaled, hidden, d_gate, d_up, out_part, in_part):
-    rows, features = tokens.shape
-    units = hidden.shape[1]
-    part = jax.ShapeDtypeStruct((n, rows, features // n), jnp.bfloat16)
-    whole = jax.ShapeDtypeStruct((n, rows, units), jnp.bfloat16)
+def exchange(n, slices, wholes, order, collective_id, cost, through=False):
+    total = len(slices) + len(wholes)
+    out_shape = [
+        jax.ShapeDtypeStruct((n, x.shape[0], x.shape[1] // n), jnp.bfloat16) for x in slices
+    ] + [jax.ShapeDtypeStruct((n,) + x.shape, jnp.bfloat16) for x in wholes]
+    if through:
+        out_shape.append(jax.ShapeDtypeStruct(slices[0].shape, jnp.bfloat16))
     outs = pl.pallas_call(
-        functools.partial(exchange_kernel, n),
-        out_shape=(part, part, whole, whole, whole),
-        in_specs=[pl.BlockSpec(memory_space=pl.ANY)] * 7,
-        out_specs=[pl.BlockSpec(memory_space=pl.ANY)] * 5,
-        scratch_shapes=[
-            pltpu.SemaphoreType.DMA((5, n)),
-            pltpu.SemaphoreType.DMA((5, n)),
-            pltpu.SemaphoreType.DMA((5, n)),
-            pltpu.SemaphoreType.DMA((5, n)),
-            pltpu.SemaphoreType.DMA((5,)),
-        ],
-        compiler_params=pltpu.CompilerParams(collective_id=0, has_side_effects=True),
-        cost_estimate=pl.CostEstimate(flops=0, bytes_accessed=300_000_000, transcendentals=0),
-    )(tokens, scaled, hidden, d_gate, d_up, out_part, in_part)
-    return [out.reshape(n * rows, out.shape[2]) for out in outs]
+        functools.partial(exchange_kernel, n, len(slices), len(wholes), len(order)),
+        out_shape=out_shape,
+        in_specs=[pl.BlockSpec(memory_space=pl.ANY)] * (total + len(order)),
+        out_specs=[pl.BlockSpec(memory_space=pl.ANY)] * len(out_shape),
+        input_output_aliases={0: total} if through else {},
+        scratch_shapes=[pltpu.SemaphoreType.DMA((total, n))] * 4
+        + [pltpu.SemaphoreType.DMA((total,))],
+        compiler_params=pltpu.CompilerParams(
+            collective_id=collective_id, has_side_effects=True
+        ),
+        cost_estimate=pl.CostEstimate(flops=0, bytes_accessed=cost, transcendentals=0),
+    )(*slices, *wholes, *order)
+    return [out.reshape(n * out.shape[1], out.shape[2]) for out in outs[:total]] + list(outs[total:])
 
 
 def local(n, tokens, expert_ids, route_probs, scale_exps, w_gate, w_up, w_down, out_grad):
@@ -159,6 +160,7 @@
     )
     scaled = (combine * out_grad.astype(jnp.float32)).astype(jnp.bfloat16)
     scaled_all = lax.all_gather(scaled, "blk", axis=0, tiled=True)
+    scaled_slice, scaled_all = exchange(n, [scaled_all], [], [], 1, 45_000_000, through=True)
     d_hidden = contract_cols(scaled_all, w_down) * scales[2]
     d_gate = (d_hidden * up_pre * sigmoid_gate * (1.0 + gate_pre * (1.0 - sigmoid_gate))).astype(
         jnp.bfloat16
@@ -170,8 +172,8 @@
     expert_out = lax.psum_scatter(out_part, "blk", scatter_dimension=0, tiled=True)
     mixed = (combine * expert_out.astype(jnp.float32)).astype(jnp.bfloat16)
     input_grad = lax.psum_scatter(in_part, "blk", scatter_dimension=0, tiled=True)
-    tokens_slice, scaled_slice, hidden_all, d_gate_all, d_up_all = exchange(
-        n, gathered, scaled_all, hidden, d_gate, d_up, out_part, in_part
+    tokens_slice, hidden_all, d_gate_all, d_up_all = exchange(
+        n, [gathered], [hidden, d_gate, d_up], [out_part, in_part, scaled_slice], 0, 300_000_000
     )
     grad_gate = contract_rows(tokens_slice, d_gate_all) * scales[0]
     grad_up = contract_rows(tokens_slice, d_up_all) * scales[1]

time: 220 us -> 204 us (0.927)
  waiting for transfers between devices: 52.8 us -> 34.3 us
  Pallas kernels: 93.6 us -> 97.1 us
    all_gather x1, waiting for transfers between devices: 22.9 us -> 4.32 us  [local(): gathered = lax.all_gather(tokens, 'blk', axis=0, tiled=True)]
    pallas_call x1 -> x2, Pallas kernels: 93.6 us -> 97.1 us  [exchange(): pl.pallas_call(functools.partial(exchange_kernel, n, len(slices), len(who...]
  transfers between devices with their start and end apart: 4 -> 4, of which waited for: 2 -> 2; matrix products, arithmetic and copies ran while one was open for 17% -> 18% of each run, Pallas kernels for 43% -> 48%
where the time goes in v4:
time: 204 us
  Pallas kernels  97.1 us (48%)
  matrix products  51.8 us (25%)
  waiting for transfers between devices  34.3 us (17%)
  between operations  13.9 us (7%)
  other arithmetic  4.87 us (2%)
    pallas_call x2, Pallas kernels, exchange(): pl.pallas_call(functools.partial(exchange_kernel, n, len(slices), len(who...  97.1 us
    all_gather x1, waiting for transfers between devices, local(): scaled_all = lax.all_gather(scaled, 'blk', axis=0, tiled=True)  29.2 us
    dot_general x3, matrix products, contract_cols(): lax.dot_general(left, right, (((1,), (1,)), ((), ())), preferred_element_...  19 us
    dot_general x3, matrix products, contract_rows(): lax.dot_general(left, right, (((0,), (0,)), ((), ())), preferred_element_...  14.6 us
    dot_general x1, matrix products, local(): jnp.dot(gathered, w_gate, preferred_element_type=jnp.float32) * scales[0]  7.24 us
    dot_general x1, matrix products, local(): jnp.dot(gathered, w_up, preferred_element_type=jnp.float32) * scales[1]  6.72 us
    all_gather x1, waiting for transfers between devices, local(): gathered = lax.all_gather(tokens, 'blk', axis=0, tiled=True)  4.32 us
    dot_general x1, matrix products, local(): jnp.dot(hidden, w_down, preferred_element_type=jnp.float32) * scales[2]  4.28 us
  transfers between devices with their start and end apart: 4, of which 2 were waited for; matrix products, arithmetic and copies ran while one was open for 18% of the time, Pallas kernels for 48%

profile of v4, /device:TPU:0, one launch (start us, length us, event | category | flops | bytes accessed | tf_op | source)
XLA Modules:
  0.0 203.8 jit_solution(10248042046112745188)
XLA Ops:
  7.2 0.0 all-gather.5.cloned.1.call-start
  7.2 0.7 fusion.6
  7.9 1.7 multiply_convert_fusion.3
  9.7 0.0 all-gather.5.cloned.1.call-update
  9.7 0.0 all-gather.3.cloned.1.call-start
  9.7 0.7 all-gather.3.cloned.1.call-update
  10.4 0.0 reduce-scatter.3.cloned.1.call-start
  10.5 0.7 multiply_exponential_fusion
  11.2 0.6 fusion.7
  11.8 29.2 %all-gather.5.cloned.1.call-done.refs_0_ = bf16[320,3072]{1,0:T(8,128)(2,1)} async-done(((bf16[40,3072]{1,0:T(8,128)(2,1)}), bf16[320,3072]{1,0:T(8,128)(2,1)}) %all-gather.5.cloned.1.call-update) | async-done | bytes 1966096 | tf_op jit(solution)/shard_map/all_gather | solution.py:162
  41.0 18.5 %shard_map.119 = (bf16[4,320,768]{2,1,0:T(8,128)(2,1)}, bf16[320,3072]{1,0:T(8,128)(2,1)}) custom-call(bf16[320,3072]{1,0:T(8,128)(2,1)} %all-gather.5.cloned.1.call-done.refs_0_), custom_call_target="tpu_custom_call", output_to_operand_aliasing={{1}: (0, {})} | custom-call | bytes 45000000 | tf_op jit(solution)/shard_map/pallas_call | solution.py:132
  59.5 6.3 %convolution_multiply_fusion.3 = f32[320,1024]{1,0:T(8,128)S(1)} fusion(bf16[320,3072]{1,0:T(8,128)(2,1)} %get-tuple-element.11, bf16[1024,3072]{1,0:T(8,128)(2,1)} %param.14, f32[]{:T(128)} %bitcast.2), kind=kOutput, calls=%fused_computation.12 | convolution fusion | flops 2013593600 | bytes 9568260 | tf_op jit(solution)/shard_map/dot_general | solution.py:18
  65.8 4.3 %all-gather.3.cloned.1.call-done.refs_0_ = bf16[320,3072]{1,0:T(8,128)(2,1)} async-done(((bf16[40,3072]{1,0:T(8,128)(2,1)}), bf16[320,3072]{1,0:T(8,128)(2,1)}) %all-gather.3.cloned.1.call-update) | async-done | bytes 1966096 | tf_op jit(solution)/shard_map/all_gather | solution.py:153
  70.2 6.7 %convolution_multiply_fusion.4 = f32[320,1024]{1,0:T(8,128)S(1)} fusion(bf16[320,3072]{1,0:T(8,128)(2,1)} %all-gather.3.cloned.1.call-done.refs_0_, bf16[3072,1024]{1,0:T(8,128)(2,1)} %param.13, f32[]{:T(128)} %bitcast.1), kind=kOutput, calls=%fused_computation.13 | convolution fusion | flops 2013593600 | bytes 9568260 | tf_op jit(solution)/shard_map/dot_general | solution.py:155
  76.9 0.0 slice-start.1
  76.9 7.2 %multiply_convert_fusion.1 = (bf16[320,1024]{1,0:T(8,128)(2,1)S(1)}, bf16[320,1024]{1,0:T(8,128)(2,1)S(1)}, bf16[320,1024]{1,0:T(8,128)(2,1)}) fusion(f32[320,1024]{1,0:T(8,128)S(1)} %convolution_multiply_fusion.3, f32[320,1024]{1,0:T(8,128)S(1)} %convolution_multiply_fusion.4, f32[]{:T(128)} %bitcast, bf16[320,3072]{1,0:T(8,128)(2,1)S(1)} %copy-done, ...), kind=kOutput, calls=%fused_computation.16 | convolution fusion | flops 2018836480 | bytes 12845060 | tf_op jit(solution)/shard_map/dot_general | solution.py:154
  84.2 0.0 slice-done
  84.2 4.3 %fusion.2.refs_4_ = bf16[320,3072]{1,0:T(8,128)(2,1)} fusion(bf16[320,1024]{1,0:T(8,128)(2,1)S(1)} %get-tuple-element.18.refs_1_, bf16[1024,3072]{1,0:T(8,128)(2,1)S(1)} %bitcast.36, f32[]{:T(128)} %bitcast.2), kind=kOutput, calls=%fused_computation.5 | convolution fusion | flops 2015232000 | bytes 8912900 | tf_op jit(solution)/shard_map/dot_general | solution.py:158
  88.5 0.0 copy-done.3
  88.5 0.0 reduce-scatter.3.cloned.1.call-update
  88.5 0.2 reduce-scatter.5.cloned.1.call-start
  88.7 0.8 copy-done.4
  89.5 5.7 %convolution_multiply_fusion = f32[320,3072]{1,0:T(8,128)S(1)} fusion(bf16[320,1024]{1,0:T(8,128)(2,1)S(1)} %copy-done.4, bf16[3072,1024]{1,0:T(8,128)(2,1)} %param.13, f32[]{:T(128)} %bitcast.1), kind=kOutput, calls=%fused_computation | convolution fusion | flops 2014248960 | bytes 10878980 | tf_op jit(solution)/shard_map/dot_general | solution.py:18
  95.2 0.0 copy-done.2
  95.2 7.0 %fusion.1.refs_5_ = bf16[320,3072]{1,0:T(8,128)(2,1)} fusion(f32[320,3072]{1,0:T(8,128)S(1)} %convolution_multiply_fusion, bf16[320,1024]{1,0:T(8,128)(2,1)S(1)} %get-tuple-element.17.refs_2_, bf16[3072,1024]{1,0:T(8,128)(2,1)} %param.12, f32[]{:T(128)} %bitcast), kind=kOutput, calls=%fused_computation.4 | convolution fusion | flops 2016215040 | bytes 12845060 | tf_op jit(solution)/shard_map/dot_general | solution.py:18
  102.2 0.0 reduce-scatter.5.cloned.1.call-update
  102.2 0.0 copy-start.1
  102.2 78.6 %shard_map.120 = (bf16[4,320,768]{2,1,0:T(8,128)(2,1)}, bf16[4,320,1024]{2,1,0:T(8,128)(2,1)}, bf16[4,320,1024]{2,1,0:T(8,128)(2,1)}, bf16[4,320,1024]{2,1,0:T(8,128)(2,1)}) custom-call(bf16[320,3072]{1,0:T(8,128)(2,1)} %all-gather.3.cloned.1.call-done.refs_0_, bf16[320,1024]{1,0:T(8,128)(2,1)} %copy-done.3, bf16[320,1024]{1,0:T(8,128)(2,1)} %copy-done.2, ...), custom_call_target="tpu_custom_call" | custom-call | bytes 300000000 | tf_op jit(solution)/shard_map/pallas_call | solution.py:132
  180.9 6.4 %fusion.3 = bf16[1024,768]{1,0:T(8,128)(2,1)} fusion(bf16[4,320,1024]{2,1,0:T(8,128)(2,1)} %get-tuple-element.16, bf16[4,320,768]{2,1,0:T(8,128)(2,1)S(1)} %copy-done.1, f32[]{:T(128)} %bitcast.2), kind=kOutput, calls=%fused_computation.7 | convolution fusion | flops 2014838784 | bytes 6160388 | tf_op jit(solution)/shard_map/dot_general | solution.py:12
  187.3 4.2 %fusion.4 = bf16[768,1024]{1,0:T(8,128)(2,1)} fusion(bf16[4,320,768]{2,1,0:T(8,128)(2,1)S(1)} %copy-done.7, bf16[4,320,1024]{2,1,0:T(8,128)(2,1)S(1)} %copy-done.6, f32[]{:T(128)} %bitcast.1), kind=kOutput, calls=%fused_computation.9 | convolution fusion | flops 2014838784 | bytes 6160388 | tf_op jit(solution)/shard_map/dot_general | solution.py:12
  191.5 4.0 %fusion.5 = bf16[768,1024]{1,0:T(8,128)(2,1)} fusion(bf16[4,320,768]{2,1,0:T(8,128)(2,1)S(1)} %copy-done.7, bf16[4,320,1024]{2,1,0:T(8,128)(2,1)S(1)} %copy-done.5, f32[]{:T(128)} %bitcast), kind=kOutput, calls=%fused_computation.11 | convolution fusion | flops 2014838784 | bytes 6160388 | tf_op jit(solution)/shard_map/dot_general | solution.py:12
  195.5 1.7 multiply_convert_fusion.4
  (17 shorter events, 0.0 us)
Async XLA Ops:
  7.2 33.8 %all-gather.5.cloned.1.call-start = ((), (), s32[]{:S(2)}) async-start(), calls=%async_computation.4 | async-start | bytes 2211840 | tf_op jit(solution)/shard_map/all_gather | solution.py:162
  9.7 60.5 %all-gather.3.cloned.1.call-start = ((), (), s32[]{:S(2)}) async-start(), calls=%async_computation.2 | async-start | bytes 2211840 | tf_op jit(solution)/shard_map/all_gather | solution.py:153
  10.4 185.0 %reduce-scatter.3.cloned.1.call-start = ((), (), s32[]{:S(2)}) async-start(), calls=%async_computation.3 | async-start | bytes 2211840 | tf_op jit(solution)/shard_map/reduce_scatter | solution.py:172
  70.2 6.7 %copy-start = (bf16[320,3072]{1,0:T(8,128)(2,1)S(1)}, bf16[320,3072]{1,0:T(8,128)(2,1)}, u32[]{:S(2)}) copy-start(bf16[320,3072]{1,0:T(8,128)(2,1)} %all-gather.3.cloned.1.call-done.refs_0_) | copy-start | bytes 5898244
  70.2 14.0 %slice-start = ((s8[6291456]{0:T(1024)(128)(4,1)}), s8[4194304]{0:T(1024)(128)(4,1)S(1)}, s32[]{:S(2)}) async-start(s8[6291456]{0:T(1024)(128)(4,1)} %bitcast.35), calls=%async_computation.6 | async-start | bytes 8388608
  76.9 7.3 %slice-start.1 = ((s8[6291456]{0:T(1024)(128)(4,1)}), s8[2097152]{0:T(1024)(128)(4,1)S(1)}, s32[]{:S(2)}) async-start(s8[6291456]{0:T(1024)(128)(4,1)} %bitcast.35), calls=%async_computation.7 | async-start | bytes 4194304
  84.2 4.3 %copy-start.3 = (bf16[320,1024]{1,0:T(8,128)(2,1)}, bf16[320,1024]{1,0:T(8,128)(2,1)S(1)}, u32[]{:S(2)}) copy-start(bf16[320,1024]{1,0:T(8,128)(2,1)S(1)} %get-tuple-element.18.refs_1_) | copy-start | bytes 1966084
  84.2 11.1 %copy-start.2 = (bf16[320,1024]{1,0:T(8,128)(2,1)}, bf16[320,1024]{1,0:T(8,128)(2,1)S(1)}, u32[]{:S(2)}) copy-start(bf16[320,1024]{1,0:T(8,128)(2,1)S(1)} %get-tuple-element.17.refs_2_) | copy-start | bytes 1966084
  88.5 1.1 copy-start.4
  88.5 108.7 %reduce-scatter.5.cloned.1.call-start = ((), (), s32[]{:S(2)}) async-start(), calls=%async_computation.5 | async-start | bytes 2211840 | tf_op jit(solution)/shard_map/reduce_scatter | solution.py:174
  102.2 78.6 %copy-start.1 = (bf16[4,320,768]{2,1,0:T(8,128)(2,1)S(1)}, bf16[4,320,768]{2,1,0:T(8,128)(2,1)}, u32[]{:S(2)}) copy-start(bf16[4,320,768]{2,1,0:T(8,128)(2,1)} %get-tuple-element.12) | copy-start | bytes 5898244
  180.8 6.4 %copy-start.6 = (bf16[4,320,1024]{2,1,0:T(8,128)(2,1)S(1)}, bf16[4,320,1024]{2,1,0:T(8,128)(2,1)}, u32[]{:S(2)}) copy-start(bf16[4,320,1024]{2,1,0:T(8,128)(2,1)} %get-tuple-element.15) | copy-start | bytes 7864324
  180.8 6.4 %copy-start.7 = (bf16[4,320,768]{2,1,0:T(8,128)(2,1)S(1)}, bf16[4,320,768]{2,1,0:T(8,128)(2,1)}, u32[]{:S(2)}) copy-start(bf16[4,320,768]{2,1,0:T(8,128)(2,1)} %get-tuple-element.13) | copy-start | bytes 5898244
  187.3 4.2 %copy-start.5 = (bf16[4,320,1024]{2,1,0:T(8,128)(2,1)S(1)}, bf16[4,320,1024]{2,1,0:T(8,128)(2,1)}, u32[]{:S(2)}) copy-start(bf16[4,320,1024]{2,1,0:T(8,128)(2,1)} %get-tuple-element.14) | copy-start | bytes 7864324
Sparse Core Ops, SparseCore 0:
  10.2 30.7 all-gather.4
  42.6 27.5 all-gather.2
  88.6 34.9 reduce-scatter.2
  126.5 33.9 reduce-scatter.4

commit v5 on v4

--- a/solution.py
+++ b/solution.py
@@ -50,19 +50,6 @@
         return pl.ds(pl.multiple_of(p * width, 128), width)
 
     sliced, sent, local = [], [], []
-    for a, (src, dst) in enumerate(slices):
-        for j in range(1, n):
-            p = (me + j) % n
-            copy = pltpu.make_async_remote_copy(
-                src_ref=src.at[my_half, columns(p)],
-                dst_ref=dst.at[me, my_half],
-                send_sem=send.at[a, j],
-                recv_sem=recv.at[a, j],
-                device_id=(p, blk),
-                device_id_type=MESH,
-            )
-            copy.start()
-            sliced.append((a, j, dst, copy))
     across, along = me + 1 - 2 * (me % 2), (me + 2) % n
     passed = []
     for a, (src, dst) in enumerate(wholes):
@@ -81,6 +68,19 @@
             copy.start()
             (passed if n == 4 else sent).append((a, j, dst, copy))
     for a, (src, dst) in enumerate(slices):
+        for j in range(1, n):
+            p = (me + j) % n
+            copy = pltpu.make_async_remote_copy(
+                src_ref=src.at[my_half, columns(p)],
+                dst_ref=dst.at[me, my_half],
+                send_sem=send.at[a, j],
+                recv_sem=recv.at[a, j],
+                device_id=(p, blk),
+                device_id_type=MESH,
+            )
+            copy.start()
+            sliced.append((a, j, dst, copy))
+    for a, (src, dst) in enumerate(slices):
         copy = pltpu.make_async_copy(src.at[:, columns(me)], dst.at[me], own.at[a])
         copy.start()
         local.append(copy)
@@ -89,19 +89,6 @@
         copy.start()
         local.append(copy)
     forwards = []
-    for a, j, dst, copy in sliced:
-        copy.wait_recv()
-        landed = dst.at[(me + n - j) % n, my_half]
-        forward = pltpu.make_async_remote_copy(
-            src_ref=landed,
-            dst_ref=landed,
-            send_sem=fsend.at[a, j],
-            recv_sem=frecv.at[a, j],
-            device_id=(me, sibling),
-            device_id_type=MESH,
-        )
-        forward.start()
-        forwards.append(forward)
     for a, j, dst, copy in passed:
         copy.wait_recv()
         owner, target = (across, along) if j == 1 else (along, across)
@@ -112,6 +99,19 @@
             send_sem=fsend.at[n_slices + a, j],
             recv_sem=frecv.at[n_slices + a, j],
             device_id=(target, blk),
+            device_id_type=MESH,
+        )
+        forward.start()
+        forwards.append(forward)
+    for a, j, dst, copy in sliced:
+        copy.wait_recv()
+        landed = dst.at[(me + n - j) % n, my_half]
+        forward = pltpu.make_async_remote_copy(
+            src_ref=landed,
+            dst_ref=landed,
+            send_sem=fsend.at[a, j],
+            recv_sem=frecv.at[a, j],
+            device_id=(me, sibling),
             device_id_type=MESH,
         )
         forward.start()

time: 204 us -> 204 us (level)
  no operation moved by 1% of the time
where the time goes in v5:
time: 204 us
  Pallas kernels  97.1 us (48%)
  matrix products  51.8 us (25%)
  waiting for transfers between devices  34.3 us (17%)
  between operations  13.9 us (7%)
  other arithmetic  4.87 us (2%)
    pallas_call x2, Pallas kernels, exchange(): pl.pallas_call(functools.partial(exchange_kernel, n, len(slices), len(who...  97.1 us
    all_gather x1, waiting for transfers between devices, local(): scaled_all = lax.all_gather(scaled, 'blk', axis=0, tiled=True)  29.2 us
    dot_general x3, matrix products, contract_cols(): lax.dot_general(left, right, (((1,), (1,)), ((), ())), preferred_element_...  19 us
    dot_general x3, matrix products, contract_rows(): lax.dot_general(left, right, (((0,), (0,)), ((), ())), preferred_element_...  14.6 us
    dot_general x1, matrix products, local(): jnp.dot(gathered, w_gate, preferred_element_type=jnp.float32) * scales[0]  7.24 us
    dot_general x1, matrix products, local(): jnp.dot(gathered, w_up, preferred_element_type=jnp.float32) * scales[1]  6.72 us
    all_gather x1, waiting for transfers between devices, local(): gathered = lax.all_gather(tokens, 'blk', axis=0, tiled=True)  4.32 us
    dot_general x1, matrix products, local(): jnp.dot(hidden, w_down, preferred_element_type=jnp.float32) * scales[2]  4.28 us
  transfers between devices with their start and end apart: 4, of which 2 were waited for; matrix products, arithmetic and copies ran while one was open for 18% of the time, Pallas kernels for 48%

profile of v5, /device:TPU:0, one launch (start us, length us, event | category | flops | bytes accessed | tf_op | source)
XLA Modules:
  0.0 203.8 jit_solution(6696052990079026860)
XLA Ops:
  7.2 0.0 all-gather.5.cloned.1.call-start
  7.2 0.7 fusion.6
  7.9 1.7 multiply_convert_fusion.3
  9.7 0.0 all-gather.5.cloned.1.call-update
  9.7 0.0 all-gather.3.cloned.1.call-start
  9.7 0.7 all-gather.3.cloned.1.call-update
  10.4 0.0 reduce-scatter.3.cloned.1.call-start
  10.5 0.7 multiply_exponential_fusion
  11.2 0.6 fusion.7
  11.8 29.2 %all-gather.5.cloned.1.call-done.refs_0_ = bf16[320,3072]{1,0:T(8,128)(2,1)} async-done(((bf16[40,3072]{1,0:T(8,128)(2,1)}), bf16[320,3072]{1,0:T(8,128)(2,1)}) %all-gather.5.cloned.1.call-update) | async-done | bytes 1966096 | tf_op jit(solution)/shard_map/all_gather | solution.py:162
  41.0 18.5 %shard_map.119 = (bf16[4,320,768]{2,1,0:T(8,128)(2,1)}, bf16[320,3072]{1,0:T(8,128)(2,1)}) custom-call(bf16[320,3072]{1,0:T(8,128)(2,1)} %all-gather.5.cloned.1.call-done.refs_0_), custom_call_target="tpu_custom_call", output_to_operand_aliasing={{1}: (0, {})} | custom-call | bytes 45000000 | tf_op jit(solution)/shard_map/pallas_call | solution.py:132
  59.5 6.3 %convolution_multiply_fusion.3 = f32[320,1024]{1,0:T(8,128)S(1)} fusion(bf16[320,3072]{1,0:T(8,128)(2,1)} %get-tuple-element.11, bf16[1024,3072]{1,0:T(8,128)(2,1)} %param.14, f32[]{:T(128)} %bitcast.2), kind=kOutput, calls=%fused_computation.12 | convolution fusion | flops 2013593600 | bytes 9568260 | tf_op jit(solution)/shard_map/dot_general | solution.py:18
  65.8 4.3 %all-gather.3.cloned.1.call-done.refs_0_ = bf16[320,3072]{1,0:T(8,128)(2,1)} async-done(((bf16[40,3072]{1,0:T(8,128)(2,1)}), bf16[320,3072]{1,0:T(8,128)(2,1)}) %all-gather.3.cloned.1.call-update) | async-done | bytes 1966096 | tf_op jit(solution)/shard_map/all_gather | solution.py:153
  70.2 6.7 %convolution_multiply_fusion.4 = f32[320,1024]{1,0:T(8,128)S(1)} fusion(bf16[320,3072]{1,0:T(8,128)(2,1)} %all-gather.3.cloned.1.call-done.refs_0_, bf16[3072,1024]{1,0:T(8,128)(2,1)} %param.13, f32[]{:T(128)} %bitcast.1), kind=kOutput, calls=%fused_computation.13 | convolution fusion | flops 2013593600 | bytes 9568260 | tf_op jit(solution)/shard_map/dot_general | solution.py:155
  76.9 0.0 copy-done
  76.9 0.0 slice-start.1
  76.9 7.2 %multiply_convert_fusion.1 = (bf16[320,1024]{1,0:T(8,128)(2,1)S(1)}, bf16[320,1024]{1,0:T(8,128)(2,1)S(1)}, bf16[320,1024]{1,0:T(8,128)(2,1)}) fusion(f32[320,1024]{1,0:T(8,128)S(1)} %convolution_multiply_fusion.3, f32[320,1024]{1,0:T(8,128)S(1)} %convolution_multiply_fusion.4, f32[]{:T(128)} %bitcast, bf16[320,3072]{1,0:T(8,128)(2,1)S(1)} %copy-done, ...), kind=kOutput, calls=%fused_computation.16 | convolution fusion | flops 2018836480 | bytes 12845060 | tf_op jit(solution)/shard_map/dot_general | solution.py:154
  84.2 0.0 slice-done
  84.2 0.0 slice-done.1
  84.2 4.3 %fusion.2.refs_4_ = bf16[320,3072]{1,0:T(8,128)(2,1)} fusion(bf16[320,1024]{1,0:T(8,128)(2,1)S(1)} %get-tuple-element.18.refs_1_, bf16[1024,3072]{1,0:T(8,128)(2,1)S(1)} %bitcast.36, f32[]{:T(128)} %bitcast.2), kind=kOutput, calls=%fused_computation.5 | convolution fusion | flops 2015232000 | bytes 8912900 | tf_op jit(solution)/shard_map/dot_general | solution.py:158
  88.5 0.0 copy-done.3
  88.5 0.0 reduce-scatter.3.cloned.1.call-update
  88.5 0.2 reduce-scatter.5.cloned.1.call-start
  88.7 0.8 copy-done.4
  89.5 5.7 %convolution_multiply_fusion = f32[320,3072]{1,0:T(8,128)S(1)} fusion(bf16[320,1024]{1,0:T(8,128)(2,1)S(1)} %copy-done.4, bf16[3072,1024]{1,0:T(8,128)(2,1)} %param.13, f32[]{:T(128)} %bitcast.1), kind=kOutput, calls=%fused_computation | convolution fusion | flops 2014248960 | bytes 10878980 | tf_op jit(solution)/shard_map/dot_general | solution.py:18
  95.2 7.0 %fusion.1.refs_5_ = bf16[320,3072]{1,0:T(8,128)(2,1)} fusion(f32[320,3072]{1,0:T(8,128)S(1)} %convolution_multiply_fusion, bf16[320,1024]{1,0:T(8,128)(2,1)S(1)} %get-tuple-element.17.refs_2_, bf16[3072,1024]{1,0:T(8,128)(2,1)} %param.12, f32[]{:T(128)} %bitcast), kind=kOutput, calls=%fused_computation.4 | convolution fusion | flops 2016215040 | bytes 12845060 | tf_op jit(solution)/shard_map/dot_general | solution.py:18
  102.2 0.0 reduce-scatter.5.cloned.1.call-update
  102.2 78.6 %shard_map.120 = (bf16[4,320,768]{2,1,0:T(8,128)(2,1)}, bf16[4,320,1024]{2,1,0:T(8,128)(2,1)}, bf16[4,320,1024]{2,1,0:T(8,128)(2,1)}, bf16[4,320,1024]{2,1,0:T(8,128)(2,1)}) custom-call(bf16[320,3072]{1,0:T(8,128)(2,1)} %all-gather.3.cloned.1.call-done.refs_0_, bf16[320,1024]{1,0:T(8,128)(2,1)} %copy-done.3, bf16[320,1024]{1,0:T(8,128)(2,1)} %copy-done.2, ...), custom_call_target="tpu_custom_call" | custom-call | bytes 300000000 | tf_op jit(solution)/shard_map/pallas_call | solution.py:132
  180.9 6.4 %fusion.3 = bf16[1024,768]{1,0:T(8,128)(2,1)} fusion(bf16[4,320,1024]{2,1,0:T(8,128)(2,1)} %get-tuple-element.16, bf16[4,320,768]{2,1,0:T(8,128)(2,1)S(1)} %copy-done.1, f32[]{:T(128)} %bitcast.2), kind=kOutput, calls=%fused_computation.7 | convolution fusion | flops 2014838784 | bytes 6160388 | tf_op jit(solution)/shard_map/dot_general | solution.py:12
  187.3 4.2 %fusion.4 = bf16[768,1024]{1,0:T(8,128)(2,1)} fusion(bf16[4,320,768]{2,1,0:T(8,128)(2,1)S(1)} %copy-done.7, bf16[4,320,1024]{2,1,0:T(8,128)(2,1)S(1)} %copy-done.6, f32[]{:T(128)} %bitcast.1), kind=kOutput, calls=%fused_computation.9 | convolution fusion | flops 2014838784 | bytes 6160388 | tf_op jit(solution)/shard_map/dot_general | solution.py:12
  191.5 4.0 %fusion.5 = bf16[768,1024]{1,0:T(8,128)(2,1)} fusion(bf16[4,320,768]{2,1,0:T(8,128)(2,1)S(1)} %copy-done.7, bf16[4,320,1024]{2,1,0:T(8,128)(2,1)S(1)} %copy-done.5, f32[]{:T(128)} %bitcast), kind=kOutput, calls=%fused_computation.11 | convolution fusion | flops 2014838784 | bytes 6160388 | tf_op jit(solution)/shard_map/dot_general | solution.py:12
  195.5 1.7 multiply_convert_fusion.4
  (17 shorter events, 0.0 us)
Async XLA Ops:
  7.2 33.8 %all-gather.5.cloned.1.call-start = ((), (), s32[]{:S(2)}) async-start(), calls=%async_computation.4 | async-start | bytes 2211840 | tf_op jit(solution)/shard_map/all_gather | solution.py:162
  9.7 60.5 %all-gather.3.cloned.1.call-start = ((), (), s32[]{:S(2)}) async-start(), calls=%async_computation.2 | async-start | bytes 2211840 | tf_op jit(solution)/shard_map/all_gather | solution.py:153
  10.4 185.0 %reduce-scatter.3.cloned.1.call-start = ((), (), s32[]{:S(2)}) async-start(), calls=%async_computation.3 | async-start | bytes 2211840 | tf_op jit(solution)/shard_map/reduce_scatter | solution.py:172
  70.2 6.7 %copy-start = (bf16[320,3072]{1,0:T(8,128)(2,1)S(1)}, bf16[320,3072]{1,0:T(8,128)(2,1)}, u32[]{:S(2)}) copy-start(bf16[320,3072]{1,0:T(8,128)(2,1)} %all-gather.3.cloned.1.call-done.refs_0_) | copy-start | bytes 5898244
  70.2 14.0 %slice-start = ((s8[6291456]{0:T(1024)(128)(4,1)}), s8[4194304]{0:T(1024)(128)(4,1)S(1)}, s32[]{:S(2)}) async-start(s8[6291456]{0:T(1024)(128)(4,1)} %bitcast.35), calls=%async_computation.6 | async-start | bytes 8388608
  76.9 7.3 %slice-start.1 = ((s8[6291456]{0:T(1024)(128)(4,1)}), s8[2097152]{0:T(1024)(128)(4,1)S(1)}, s32[]{:S(2)}) async-start(s8[6291456]{0:T(1024)(128)(4,1)} %bitcast.35), calls=%async_computation.7 | async-start | bytes 4194304
  84.2 4.3 %copy-start.3 = (bf16[320,1024]{1,0:T(8,128)(2,1)}, bf16[320,1024]{1,0:T(8,128)(2,1)S(1)}, u32[]{:S(2)}) copy-start(bf16[320,1024]{1,0:T(8,128)(2,1)S(1)} %get-tuple-element.18.refs_1_) | copy-start | bytes 1966084
  84.2 11.1 %copy-start.2 = (bf16[320,1024]{1,0:T(8,128)(2,1)}, bf16[320,1024]{1,0:T(8,128)(2,1)S(1)}, u32[]{:S(2)}) copy-start(bf16[320,1024]{1,0:T(8,128)(2,1)S(1)} %get-tuple-element.17.refs_2_) | copy-start | bytes 1966084
  88.5 1.1 copy-start.4
  88.5 108.8 %reduce-scatter.5.cloned.1.call-start = ((), (), s32[]{:S(2)}) async-start(), calls=%async_computation.5 | async-start | bytes 2211840 | tf_op jit(solution)/shard_map/reduce_scatter | solution.py:174
  102.2 78.6 %copy-start.1 = (bf16[4,320,768]{2,1,0:T(8,128)(2,1)S(1)}, bf16[4,320,768]{2,1,0:T(8,128)(2,1)}, u32[]{:S(2)}) copy-start(bf16[4,320,768]{2,1,0:T(8,128)(2,1)} %get-tuple-element.12) | copy-start | bytes 5898244
  180.8 6.4 %copy-start.6 = (bf16[4,320,1024]{2,1,0:T(8,128)(2,1)S(1)}, bf16[4,320,1024]{2,1,0:T(8,128)(2,1)}, u32[]{:S(2)}) copy-start(bf16[4,320,1024]{2,1,0:T(8,128)(2,1)} %get-tuple-element.15) | copy-start | bytes 7864324
  180.8 6.4 %copy-start.7 = (bf16[4,320,768]{2,1,0:T(8,128)(2,1)S(1)}, bf16[4,320,768]{2,1,0:T(8,128)(2,1)}, u32[]{:S(2)}) copy-start(bf16[4,320,768]{2,1,0:T(8,128)(2,1)} %get-tuple-element.13) | copy-start | bytes 5898244
  187.3 4.2 %copy-start.5 = (bf16[4,320,1024]{2,1,0:T(8,128)(2,1)S(1)}, bf16[4,320,1024]{2,1,0:T(8,128)(2,1)}, u32[]{:S(2)}) copy-start(bf16[4,320,1024]{2,1,0:T(8,128)(2,1)} %get-tuple-element.14) | copy-start | bytes 7864324
Sparse Core Ops, SparseCore 0:
  10.2 30.7 all-gather.4
  42.6 27.5 all-gather.2
  88.6 35.0 reduce-scatter.2
  126.5 33.8 reduce-scatter.4
